TPU v7x, 32 devices: a whole 2x2x4 slice. The times are simulated.
32 devices in a mesh: group: 2 (over y), tensor: 4 (over z), dp: 4 (over x, core).
Axes of the slice: x: 2, y: 2, z: 4, core: 2. Of those that a mesh axis runs over, the one named last changes fastest.
Arguments:
- tokens: float32 [1920, 4096], P(('group', 'dp'), 'tensor'), parts along dimension 0, may hold values from -6 to 6
- cotangent: float32 [1920, 4096], P(('group', 'dp'), 'tensor'), parts along dimension 0, may hold values from -6 to 6
- w_up: float32 [288, 256, 256], P('tensor', 'dp'), may hold values from -0.1875 to 0.1875
- w_down: float32 [288, 256, 256], P('tensor', 'dp'), may hold values from -0.09375 to 0.09375
- block_col: int32 [4, 72], P('tensor'), may hold values from 0 to 15, as said below
- block_row: int32 [4, 72], P('tensor'), may hold values from 0 to 15
- block_count: int32 [4], P('tensor'), may hold values from 56 to 72, as said below
Outputs:
- mixed: float32 [1920, 4096], P(('group', 'dp'), 'tensor'), parts along dimension 0
- grad_tokens: float32 [1920, 4096], P(('group', 'dp'), 'tensor'), parts along dimension 0
- grad_up: float32 [576, 256, 256], P(('group', 'tensor'), 'dp'), parts along dimension 0
- grad_down: float32 [576, 256, 256], P(('group', 'tensor'), 'dp'), parts along dimension 0
There are 2 independent parts, one for each index of `group`. A program takes and returns all parts, laid end to end along the dimension named above; an argument that names none is the same for every part. Nothing has to cross between parts.
Inputs may be any that keep to these rules, and one draw needn't show every extreme that they name: `block_col`: hidden block of each slot; within one index of tensor the first live slots name distinct pairs of hidden and model block. `block_count`: some index of tensor has all 72 slots live in every draw; the others have fewer or as many.
All inputs are finite; a program needn't handle non-finite values.
Results may differ from a plain program's by a relative error of at most 0.00013.
Values sent between devices are 32-bit elements; how exact they have to be, the bound alone decides.
A program may use at most 320 MiB of HBM per device.

v0:
```python
import jax
import jax.numpy as jnp
from jax import lax
from jax.sharding import PartitionSpec as P

FF = 16384


precise = lax.Precision.HIGHEST


def gelu_tanh(values):
    return jax.nn.gelu(values, approximate=True)


def on_device(tokens, cotangent, w_up, w_down, block_col, block_row, block_count):
    rows_here = tokens.shape[0]
    block_size = w_up.shape[2]
    full_tokens, full_upstream = (
        lax.all_gather(tokens, "tensor", axis=1, tiled=True),
        lax.all_gather(cotangent, "tensor", axis=1, tiled=True),
    )
    width = full_tokens.shape[1]
    model_blocks = width // block_size
    hidden_blocks = FF // (block_size * lax.axis_size("tensor"))
    slot_cols = block_col[0]
    slot_rows = block_row[0]
    slot_num = slot_cols.shape[0]
    alive_slots = (lax.iota(jnp.int32, slot_num) < block_count[0]).astype(jnp.float32)
    col_onehot = (slot_cols[:, None] == lax.iota(jnp.int32, hidden_blocks)[None, :]).astype(
        jnp.float32
    ) * alive_slots[:, None]
    row_onehot = (slot_rows[:, None] == lax.iota(jnp.int32, model_blocks)[None, :]).astype(
        jnp.float32
    ) * alive_slots[:, None]
    up_tiles, down_tiles = (
        lax.all_gather(w_up, "dp", axis=1, tiled=True),
        lax.all_gather(w_down, "dp", axis=1, tiled=True),
    )
    picked = jnp.einsum(
        "trb,sr->tsb",
        full_tokens.reshape(rows_here, model_blocks, block_size),
        row_onehot,
        precision=precise,
    )
    upper = jnp.einsum("tsb,sbe->tse", picked, up_tiles, precision=precise)
    hidden = jnp.einsum("tse,sf->tfe", upper, col_onehot, precision=precise)
    activ, gelu_pull = jax.vjp(gelu_tanh, hidden)
    act_pick = jnp.einsum("tfe,sf->tse", activ, col_onehot, precision=precise)
    down_terms = jnp.einsum("tse,sed->tsd", act_pick, down_tiles, precision=precise)
    partial_out = jnp.einsum("tsd,sr->trd", down_terms, row_onehot, precision=precise).reshape(
        rows_here, width
    )
    mixed_out = lax.psum_scatter(partial_out, "tensor", scatter_dimension=1, tiled=True)
    back_up, back_down = (up_tiles, down_tiles)
    upstream_pick = jnp.einsum(
        "trd,sr->tsd",
        full_upstream.reshape(rows_here, model_blocks, block_size),
        row_onehot,
        precision=precise,
    )
    grad_down_full = jnp.einsum("tse,tsd->sed", act_pick, upstream_pick, precision=precise)
    grad_pick = jnp.einsum("tsd,sed->tse", upstream_pick, back_down, precision=precise)
    grad_activ = jnp.einsum("tse,sf->tfe", grad_pick, col_onehot, precision=precise)
    grad_hidden = gelu_pull(grad_activ)[0]
    grad_upper = jnp.einsum("tfe,sf->tse", grad_hidden, col_onehot, precision=precise)
    grad_up_full = jnp.einsum("tsb,tse->sbe", picked, grad_upper, precision=precise)
    grad_picked = jnp.einsum("tse,sbe->tsb", grad_upper, back_up, precision=precise)
    grad_whole = jnp.einsum("tsb,sr->trb", grad_picked, row_onehot, precision=precise).reshape(
        rows_here, width
    )
    grad_tokens = lax.psum_scatter(grad_whole, "tensor", scatter_dimension=1, tiled=True)
    grad_up, grad_down = (
        lax.psum_scatter(grad_up_full, "dp", scatter_dimension=1, tiled=True),
        lax.psum_scatter(grad_down_full, "dp", scatter_dimension=1, tiled=True),
    )
    return (mixed_out, grad_tokens, grad_up, grad_down)


def solution(mesh):
    in_specs = (
        P(("group", "dp"), "tensor"),
        P(("group", "dp"), "tensor"),
        P("tensor", "dp", None),
        P("tensor", "dp", None),
        P("tensor", None),
        P("tensor", None),
        P("tensor"),
    )
    out_specs = (
        P(("group", "dp"), "tensor"),
        P(("group", "dp"), "tensor"),
        P(("group", "tensor"), "dp", None),
        P(("group", "tensor"), "dp", None),
    )
    return jax.shard_map(
        on_device, mesh=mesh, in_specs=in_specs, out_specs=out_specs, check_vma=False
    )
```

profile of v0, /device:TPU:0, one launch (start us, length us, event | category | flops | bytes accessed | tf_op | source)
XLA Modules:
  0.0 970.0 jit_solution(10672689197064390774)
XLA Ops:
  10.7 78.1 %all-gather.5.cloned.1.call-done = f32[240,4096]{1,0:T(8,128)} async-done(((f32[240,1024]{1,0:T(8,128)}), f32[240,4096]{1,0:T(8,128)}) %all-gather.5.cloned.1.call-update) | async-done | bytes 3932176 | tf_op jit(solution)/shard_map/all_gather | solution.py:20
  88.8 5.6 copy.19
  94.4 71.0 %all-gather.11.cloned.1.call-done = f32[240,4096]{1,0:T(8,128)} async-done(((f32[240,1024]{1,0:T(8,128)}), f32[240,4096]{1,0:T(8,128)}) %all-gather.11.cloned.1.call-update) | async-done | bytes 3932176 | tf_op jit(solution)/shard_map/all_gather | solution.py:21
  165.4 3.7 copy.21
  169.1 18.4 %convolution_bitcast_fusion.3 = f32[240,72,256]{2,1,0:T(8,128)} fusion(f32[240,16,256]{2,1,0:T(8,128)} %bitcast.93, f32[72]{0:T(128)S(1)} %compare_convert_fusion, s32[72]{0:T(128)S(1)} %bitcast.99), kind=kOutput, calls=%fused_computation.29 | convolution fusion | flops 849348864 | bytes 21627456 | tf_op jit(solution)/shard_map/trb,sr->tsb/dot_general | solution.py:40
  187.5 16.9 %convolution_bitcast_fusion.1 = f32[240,72,256]{2,1,0:T(8,128)} fusion(f32[240,16,256]{2,1,0:T(8,128)S(1)} %bitcast.94, f32[72]{0:T(128)S(1)} %compare_convert_fusion, s32[72]{0:T(128)S(1)} %bitcast.100), kind=kOutput, calls=%fused_computation.27 | convolution fusion | flops 849348864 | bytes 21627456 | tf_op jit(solution)/shard_map/trd,sr->tsd/dot_general | solution.py:56
  204.4 81.1 %all-gather.7.cloned.1.call-done = f32[72,256,256]{2,1,0:T(8,128)} async-done(((f32[72,64,256]{2,1,0:T(8,128)}), f32[72,256,256]{2,1,0:T(8,128)}) %all-gather.7.cloned.1.call-update) | async-done | bytes 18874384 | tf_op jit(solution)/shard_map/all_gather | solution.py:37
  285.6 33.0 %fusion.23 = f32[72,240,256]{2,1,0:T(8,128)} fusion(f32[72,256,256]{2,1,0:T(8,128)} %all-gather.7.cloned.1.call-done, f32[240,72,256]{2,1,0:T(8,128)} %convolution_bitcast_fusion.3), kind=kOutput, calls=%fused_computation.23 | convolution fusion | flops 13589544960 | bytes 54263808 | tf_op jit(solution)/shard_map/tsb,sbe->tse/dot_general | solution.py:46
  318.6 24.8 %fusion.6 = f32[16,240,256]{2,0,1:T(8,128)S(1)} fusion(f32[72,240,256]{2,1,0:T(8,128)} %fusion.23, s32[72]{0:T(128)S(1)} %bitcast.103, f32[72]{0:T(128)S(1)} %compare_convert_fusion), kind=kOutput, calls=%fused_computation.6 | convolution fusion | flops 849348864 | bytes 21627456 | tf_op jit(solution)/shard_map/tse,sf->tfe/dot_general | solution.py:47
  345.4 17.0 %convolution_bitcast_fusion.2 = f32[240,72,256]{2,1,0:T(8,128)} fusion(f32[16,240,256]{2,0,1:T(8,128)S(1)} %fusion.6, s32[72]{0:T(128)S(1)} %bitcast.104, f32[72]{0:T(128)S(1)} %compare_convert_fusion), kind=kOutput, calls=%fused_computation.28 | convolution fusion | flops 857213184 | bytes 21627456 | tf_op jit(solution)/shard_map/tfe,sf->tse/dot_general | solution.py:49
  362.4 44.7 %all-gather.9.cloned.1.call-done = f32[72,256,256]{2,1,0:T(8,128)} async-done(((f32[72,64,256]{2,1,0:T(8,128)}), f32[72,256,256]{2,1,0:T(8,128)}) %all-gather.9.cloned.1.call-update) | async-done | bytes 18874384 | tf_op jit(solution)/shard_map/all_gather | solution.py:38
  407.0 31.1 %fusion.16 = f32[72,240,256]{2,1,0:T(8,128)} fusion(f32[72,256,256]{2,1,0:T(8,128)} %all-gather.9.cloned.1.call-done, f32[240,72,256]{2,1,0:T(8,128)} %convolution_bitcast_fusion.2), kind=kOutput, calls=%fused_computation.16 | convolution fusion | flops 13589544960 | bytes 54263808 | tf_op jit(solution)/shard_map/tse,sed->tsd/dot_general | solution.py:50
  438.1 24.6 %fusion.4 = f32[16,240,256]{2,0,1:T(8,128)S(1)} fusion(f32[72,240,256]{2,1,0:T(8,128)} %fusion.16, f32[72]{0:T(128)S(1)} %compare_convert_fusion, s32[72]{0:T(128)S(1)} %bitcast.101), kind=kOutput, calls=%fused_computation.4 | convolution fusion | flops 849348864 | bytes 21627456 | tf_op jit(solution)/shard_map/tsd,sr->trd/dot_general | solution.py:51
  462.7 5.4 copy.20
  468.2 31.5 %fusion.12 = f32[72,240,256]{2,1,0:T(8,128)} fusion(f32[72,256,256]{2,1,0:T(8,128)} %all-gather.9.cloned.1.call-done, f32[240,72,256]{2,1,0:T(8,128)} %convolution_bitcast_fusion.1), kind=kOutput, calls=%fused_computation.12 | convolution fusion | flops 13589544960 | bytes 54263808 | tf_op jit(solution)/shard_map/tsd,sed->tse/dot_general | solution.py:63
  499.7 25.2 %fusion.2 = f32[16,240,256]{2,0,1:T(8,128)S(1)} fusion(f32[72,240,256]{2,1,0:T(8,128)} %fusion.12, s32[72]{0:T(128)S(1)} %bitcast.105, f32[72]{0:T(128)S(1)} %compare_convert_fusion), kind=kOutput, calls=%fused_computation.2 | convolution fusion | flops 849348864 | bytes 21627456 | tf_op jit(solution)/shard_map/tse,sf->tfe/dot_general | solution.py:64
  524.9 17.7 %convolution_bitcast_fusion = f32[240,72,256]{2,1,0:T(8,128)} fusion(f32[16,240,256]{2,0,1:T(8,128)S(1)} %fusion.2, f32[16,240,256]{2,0,1:T(8,128)S(1)} %copy-done.1, s32[72]{0:T(128)S(1)} %bitcast.106, f32[72]{0:T(128)S(1)} %compare_convert_fusion), kind=kOutput, calls=%fused_computation.26 | convolution fusion | flops 868026624 | bytes 25559616 | tf_op jit(solution)/shard_map/tfe,sf->tse/dot_general | solution.py:66
  542.6 31.4 %fusion.19 = f32[72,240,256]{2,1,0:T(8,128)} fusion(f32[72,256,256]{2,1,0:T(8,128)} %all-gather.7.cloned.1.call-done, f32[240,72,256]{2,1,0:T(8,128)} %convolution_bitcast_fusion), kind=kOutput, calls=%fused_computation.19 | convolution fusion | flops 13589544960 | bytes 54263808 | tf_op jit(solution)/shard_map/tse,sbe->tsb/dot_general | solution.py:68
  574.0 24.7 %fusion = f32[16,240,256]{2,0,1:T(8,128)S(1)} fusion(f32[72,240,256]{2,1,0:T(8,128)} %fusion.19, f32[72]{0:T(128)S(1)} %compare_convert_fusion, s32[72]{0:T(128)S(1)} %bitcast.102), kind=kOutput, calls=%fused_computation | convolution fusion | flops 849348864 | bytes 21627456 | tf_op jit(solution)/shard_map/tsb,sr->trb/dot_general | solution.py:69
  598.8 5.4 copy.22
  604.3 62.8 %fusion.21 = f32[72,256,256]{2,1,0:T(8,128)} fusion(f32[240,72,256]{2,1,0:T(8,128)} %convolution_bitcast_fusion, f32[240,72,256]{2,1,0:T(8,128)} %convolution_bitcast_fusion.3), kind=kOutput, calls=%fused_computation.21 | convolution fusion | flops 13589544960 | bytes 54263808 | tf_op jit(solution)/shard_map/tsb,tse->sbe/dot_general | solution.py:67
  667.1 52.1 %fusion.14 = f32[72,256,256]{2,1,0:T(8,128)} fusion(f32[240,72,256]{2,1,0:T(8,128)} %convolution_bitcast_fusion.1, f32[240,72,256]{2,1,0:T(8,128)} %convolution_bitcast_fusion.2), kind=kOutput, calls=%fused_computation.14 | convolution fusion | flops 13589544960 | bytes 54263808 | tf_op jit(solution)/shard_map/tse,tsd->sed/dot_general | solution.py:62
  719.3 100.8 %reduce-scatter.9.cloned.1.call-done = f32[72,64,256]{2,1,0:T(8,128)} async-done(((f32[72,256,256]{2,1,0:T(8,128)}), f32[72,64,256]{2,1,0:T(8,128)}) %reduce-scatter.9.cloned.1.call-update) | async-done | bytes 4718608 | tf_op jit(solution)/shard_map/reduce_scatter | solution.py:74
  820.1 142.8 %reduce-scatter.11.cloned.1.call-done = f32[72,64,256]{2,1,0:T(8,128)} async-done(((f32[72,256,256]{2,1,0:T(8,128)}), f32[72,64,256]{2,1,0:T(8,128)}) %reduce-scatter.11.cloned.1.call-update) | async-done | bytes 4718608 | tf_op jit(solution)/shard_map/reduce_scatter | solution.py:75
  (27 shorter events, 4.9 us)
Async XLA Ops:
  7.2 161.9 %copy-start.2 = (s32[1,72]{1,0:T(1,128)S(1)}, s32[1,72]{1,0:T(1,128)}, u32[]{:S(2)}) copy-start(s32[1,72]{1,0:T(1,128)} %param.12) | copy-start | bytes 868
  7.2 81.6 %all-gather.5.cloned.1.call-start = ((), (), s32[]{:S(2)}) async-start(), calls=%async_computation.4 | async-start | bytes 4915200 | tf_op jit(solution)/shard_map/all_gather | solution.py:20
  7.9 157.5 %all-gather.11.cloned.1.call-start = ((), (), s32[]{:S(2)}) async-start(), calls=%async_computation.8 | async-start | bytes 4915200 | tf_op jit(solution)/shard_map/all_gather | solution.py:21
  8.7 276.9 %all-gather.7.cloned.1.call-start = ((), (), s32[]{:S(2)}) async-start(), calls=%async_computation.5 | async-start | bytes 23592960 | tf_op jit(solution)/shard_map/all_gather | solution.py:37
  9.4 397.6 %all-gather.9.cloned.1.call-start = ((), (), s32[]{:S(2)}) async-start(), calls=%async_computation.6 | async-start | bytes 23592960 | tf_op jit(solution)/shard_map/all_gather | solution.py:38
  10.0 709.3 %reduce-scatter.5.cloned.1.call-start = ((), (), s32[]{:S(2)}) async-start(), calls=%async_computation.7 | async-start | bytes 4915200 | tf_op jit(solution)/shard_map/reduce_scatter | solution.py:54
  204.4 114.2 %copy-start.3 = (s32[1,72]{1,0:T(1,128)S(1)}, s32[1,72]{1,0:T(1,128)}, u32[]{:S(2)}) copy-start(s32[1,72]{1,0:T(1,128)} %param.11) | copy-start | bytes 868
  343.4 1.9 copy-start
  468.1 251.2 %reduce-scatter.7.cloned.1.call-start = ((), (), s32[]{:S(2)}) async-start(), calls=%async_computation.9 | async-start | bytes 4915200 | tf_op jit(solution)/shard_map/reduce_scatter | solution.py:72
  499.7 25.2 %copy-start.1 = (f32[16,240,256]{2,0,1:T(8,128)S(1)}, f32[16,240,256]{2,0,1:T(8,128)}, u32[]{:S(2)}) copy-start(f32[16,240,256]{2,0,1:T(8,128)} %copy-done) | copy-start | bytes 11796484
  604.3 215.9 %reduce-scatter.9.cloned.1.call-start = ((), (), s32[]{:S(2)}) async-start(), calls=%async_computation.10 | async-start | bytes 23592960 | tf_op jit(solution)/shard_map/reduce_scatter | solution.py:74
  667.1 295.9 %reduce-scatter.11.cloned.1.call-start = ((), (), s32[]{:S(2)}) async-start(), calls=%async_computation.11 | async-start | bytes 23592960 | tf_op jit(solution)/shard_map/reduce_scatter | solution.py:75
Sparse Core Ops, SparseCore 0:
  9.6 79.1 all-gather.4
  90.3 74.9 all-gather.10
  166.9 118.5 all-gather.6
  287.0 120.0 all-gather.8
  468.3 72.6 reduce-scatter.4
  604.4 72.6 reduce-scatter.6
  680.3 139.8 reduce-scatter.8
  823.5 139.4 reduce-scatter.10
where the time goes:
time: 974 us; the launch traced here: 970 us
  waiting for transfers between devices  521 us (53%)
  matrix products  411 us (42%)
  local copies, waits for them, and re-layouts  22.1 us (2%)
  between operations  15.1 us (2%)
    reduce_scatter x1, waiting for transfers between devices, on_device(): lax.psum_scatter(grad_down_full, 'dp', scatter_dimension=1, tiled=True)  143 us
    reduce_scatter x1, waiting for transfers between devices, on_device(): lax.psum_scatter(grad_up_full, 'dp', scatter_dimension=1, tiled=True)  101 us
    all_gather x1, waiting for transfers between devices, on_device(): lax.all_gather(w_up, 'dp', axis=1, tiled=True)  81.1 us
    all_gather x1, waiting for transfers between devices, on_device(): lax.all_gather(tokens, 'tensor', axis=1, tiled=True)  78.1 us
    all_gather x1, waiting for transfers between devices, on_device(): lax.all_gather(cotangent, 'tensor', axis=1, tiled=True)  71 us
    dot_general x1, matrix products, on_device(): jnp.einsum('tsb,tse->sbe', picked, grad_upper, precision=precise)  62.8 us
    dot_general x1, matrix products, on_device(): jnp.einsum('tse,tsd->sed', act_pick, upstream_pick, precision=precise)  52.1 us
    all_gather x1, waiting for transfers between devices, on_device(): lax.all_gather(w_down, 'dp', axis=1, tiled=True)  44.7 us
  transfers between devices with their start and end apart: 8, of which 6 were waited for; matrix products, arithmetic and copies ran while one was open for 38% of the time, Pallas kernels for 0%

commit v1 on v0

v1 whole, which is shorter than its diff:
```python
import functools

import jax
import jax.numpy as jnp
from jax import lax
from jax.experimental import pallas as pl
from jax.experimental.pallas import tpu as pltpu
from jax.sharding import PartitionSpec as P

FF = 16384
CUBIC = 0.044715
SCALE = 0.7978845608028654
F32 = jnp.float32
BF16 = jnp.bfloat16


def split(v):
    high = v.astype(BF16)
    return high, (v - high.astype(F32)).astype(BF16)


def mm(a, b, ca, cb):
    dims = (((ca,), (cb,)), ((), ()))
    dot = functools.partial(lax.dot_general, dimension_numbers=dims, preferred_element_type=F32)
    return dot(a[0], b[0]) + (dot(a[0], b[1]) + dot(a[1], b[0]))


def feature(ref, block, per, size):
    if per == 1:
        return ref.at[block]
    at = pl.multiple_of((block % per) * size, size)
    return ref.at[block // per, :, pl.ds(at, size)]


def fill(refs, inits):
    for ref, init in zip(refs, inits):
        def one(i, carry, ref=ref, init=init):
            ref[i] = jnp.zeros(ref.shape[1:], ref.dtype) if init is None else init[i]
            return carry

        lax.fori_loop(0, ref.shape[0], one, 0)


def load_tile(pieces, offs, j, high, low):
    for p, piece in enumerate(pieces):
        rows = piece.shape[1]
        h, l = split(piece[j])
        at = pl.ds(pl.multiple_of(offs[p], rows), rows)
        high[j, at, :] = h
        low[j, at, :] = l
    return high[j], low[j]


def up_kernel(cfg, table, offs, tok, *refs):
    base, n, per, size, pieces_n, first, final = cfg
    pieces, refs = refs[:pieces_n], refs[pieces_n:]
    init = None
    if not first:
        init, refs = refs[0], refs[1:]
    if final:
        act, slope, high, low, acc = refs
    else:
        acc, high, low = refs
    step = pl.program_id(0)

    @pl.when(step == 0)
    def _():
        fill([acc], [init])

    for j in range(n):
        s = base + step * n + j
        q, r = table[0, s], table[1, s]
        live = jnp.where(s < table[2, 0], 1.0, 0.0).astype(F32)
        tile = load_tile(pieces, offs, j, high, low)
        acc[q] += live * mm(split(feature(tok, r, per, size)[...]), tile, 1, 0)

    if final:
        @pl.when(step == pl.num_programs(0) - 1)
        def _():
            def one(i, carry):
                v = acc[i]
                t = jnp.tanh(SCALE * (v + CUBIC * (v * v * v)))
                act[i] = 0.5 * v * (1.0 + t)
                slope[i] = 0.5 * (1.0 + t) + (0.5 * SCALE) * v * (1.0 - t * t) * (
                    1.0 + (3.0 * CUBIC) * (v * v)
                )
                return carry

            lax.fori_loop(0, acc.shape[0], one, 0)


def emit_grad(out_pieces, offs, start, j, g_scr, g):
    g_scr[j] = g
    for p, out in enumerate(out_pieces):
        rows = out.shape[1]
        out[j] = g_scr[j, pl.ds(pl.multiple_of(offs[start + p], rows), rows), :]


def down_kernel(cfg, out_n, table, offs, act, slope, cot, *refs):
    base, n, per, size, pieces_n, first, final = cfg
    pieces, refs = refs[:pieces_n], refs[pieces_n:]
    inits = (None, None)
    if not first:
        inits, refs = refs[:2], refs[2:]
    mixed, back = refs[:2]
    outs, (high, low, g_scr) = refs[2:2 + out_n], refs[2 + out_n:]
    step = pl.program_id(0)

    @pl.when(step == 0)
    def _():
        fill([mixed, back], inits)

    for j in range(n):
        s = base + step * n + j
        q, r = table[0, s], table[1, s]
        live = jnp.where(s < table[2, 0], 1.0, 0.0).astype(F32)
        tile = load_tile(pieces, offs, j, high, low)
        a = split(act[q])
        b = split(feature(cot, r, per, size)[...])
        emit_grad(outs, offs, pieces_n, j, g_scr, live * mm(a, b, 0, 0))
        back[q] += live * mm(b, tile, 1, 1)
        place = feature(mixed, r, per, size)
        place[...] += live * mm(a, tile, 1, 0)

    if final:
        @pl.when(step == pl.num_programs(0) - 1)
        def _():
            def one(i, carry):
                back[i] = back[i] * slope[i]
                return carry

            lax.fori_loop(0, back.shape[0], one, 0)


def end_kernel(cfg, out_n, table, offs, tok, gh, *refs):
    base, n, per, size, pieces_n, first, final = cfg
    pieces, refs = refs[:pieces_n], refs[pieces_n:]
    init = None
    if not first:
        init, refs = refs[0], refs[1:]
    grad = refs[0]
    outs, (high, low, g_scr) = refs[1:1 + out_n], refs[1 + out_n:]
    step = pl.program_id(0)

    @pl.when(step == 0)
    def _():
        fill([grad], [init])

    for j in range(n):
        s = base + step * n + j
        q, r = table[0, s], table[1, s]
        live = jnp.where(s < table[2, 0], 1.0, 0.0).astype(F32)
        tile = load_tile(pieces, offs, j, high, low)
        a = split(feature(tok, r, per, size)[...])
        b = split(gh[q])
        emit_grad(outs, offs, pieces_n, j, g_scr, live * mm(a, b, 0, 0))
        place = feature(grad, r, per, size)
        place[...] += live * mm(b, tile, 1, 1)


def call(kernel, table, offs, whole_in, pieces, inits, whole_out, out_rows, n, size, scratch, flops):
    slots = pieces[0].shape[0]

    def whole(shape):
        return pl.BlockSpec(shape, lambda i, *_: (0,) * len(shape), pipeline_mode=pl.Buffered(1))

    def part(rows):
        return pl.BlockSpec((n, rows, size), lambda i, *_: (i, 0, 0))

    args = list(whole_in) + list(pieces) + list(inits)
    moved = sum(a.size for a in args) * 4 + 4 * sum(
        slots * rows * size for rows in out_rows
    ) + 4 * sum(functools.reduce(lambda x, y: x * y, s) for s in whole_out)
    return pl.pallas_call(
        kernel,
        grid_spec=pltpu.PrefetchScalarGridSpec(
            num_scalar_prefetch=2,
            grid=(slots // n,),
            in_specs=[whole(a.shape) for a in whole_in]
            + [part(p.shape[1]) for p in pieces]
            + [whole(a.shape) for a in inits],
            out_specs=[whole(s) for s in whole_out] + [part(rows) for rows in out_rows],
            scratch_shapes=scratch,
        ),
        out_shape=[jax.ShapeDtypeStruct(s, F32) for s in whole_out]
        + [jax.ShapeDtypeStruct((slots, rows, size), F32) for rows in out_rows],
        compiler_params=pltpu.CompilerParams(
            dimension_semantics=("arbitrary",), vmem_limit_bytes=56 * 1024 * 1024
        ),
        cost_estimate=pl.CostEstimate(flops=flops, bytes_accessed=moved, transcendentals=0),
    )(table, offs, *args)


def on_device(groups, dps, tokens, cotangent, w_up, w_down, block_col, block_row, block_count):
    slots, rows_w, size = w_up.shape
    rows, width = tokens.shape
    tensor = lax.axis_size("tensor")
    per = width // size
    hidden = FF // (size * tensor)
    paired = groups == 2 and dps == 4 and slots % 8 == 0
    chunks = 2 if paired else 1
    count = slots // chunks
    n = max(k for k in (1, 2, 3, 4) if count % k == 0)

    table = jnp.stack([block_col[0], block_row[0], jnp.broadcast_to(block_count, (slots,))])
    d = lax.axis_index("dp")
    if paired:
        y = lax.axis_index("group")
        half = rows_w // 2
        other_core, other_x = d + 1 - 2 * (d % 2), (d + 2) % 4
        other_both = other_core + 2 - 4 * (other_core // 2)

        def over_core(v):
            return lax.ppermute(v, "dp", [(0, 1), (1, 0), (2, 3), (3, 2)])

        def over_x(v):
            return lax.ppermute(v, "dp", [(0, 2), (2, 0), (1, 3), (3, 1)])

        def over_y(v):
            return lax.ppermute(v, "group", [(0, 1), (1, 0)])

        def gather(w):
            near = lax.dynamic_slice_in_dim(w, y * half, half, axis=1)
            by_x = over_x(near)
            by_y = over_y(by_x)
            return (w, over_core(w), by_x, by_y, over_core(by_x), over_core(by_y))

        offs = jnp.stack(
            [
                d * rows_w,
                other_core * rows_w,
                other_x * rows_w + y * half,
                other_x * rows_w + (1 - y) * half,
                other_both * rows_w + y * half,
                other_both * rows_w + (1 - y) * half,
                d * rows_w,
                other_x * rows_w,
                other_core * rows_w,
                other_both * rows_w,
            ]
        ).astype(jnp.int32)
        out_rows = (rows_w,) * 4

        def scatter(mine, to_x, to_core, to_both):
            far = over_x(to_x + over_core(to_both))
            return mine + over_core(to_core), far
    else:
        offs = jnp.zeros((2,), jnp.int32)
        out_rows = (size,)

        def gather(w):
            return (lax.all_gather(w, "dp", axis=1, tiled=True),)

        def scatter(whole):
            return (lax.psum_scatter(whole, "dp", scatter_dimension=1, tiled=True),)

    full_tokens = lax.all_gather(tokens, "tensor")
    ups = [gather(w_up[c * count:(c + 1) * count]) for c in range(chunks)]
    downs = [gather(w_down[c * count:(c + 1) * count]) for c in range(chunks)]
    full_cot = lax.all_gather(cotangent, "tensor")

    acts = (hidden, rows, size)
    feats = (tensor, rows, width)
    tiles = [pltpu.VMEM((n, size, size), BF16), pltpu.VMEM((n, size, size), BF16)]
    g_tile = [pltpu.VMEM((n, size, size), F32)]
    product = 6 * count * rows * size * size

    def cfg(c):
        return (c * count, n, per, size, len(ups[c]), c == 0, c == chunks - 1)

    state = []
    for c in range(chunks):
        last = c == chunks - 1
        state = call(
            functools.partial(up_kernel, cfg(c)), table, offs, [full_tokens], ups[c], state,
            [acts, acts] if last else [acts], (), n, size,
            tiles + ([pltpu.VMEM(acts, F32)] if last else []), product,
        )
    act, slope = state

    state, down_grads = [], []
    for c in range(chunks):
        mixed, back, *parts = call(
            functools.partial(down_kernel, cfg(c), len(out_rows)), table, offs,
            [act, slope, full_cot], downs[c], state, [feats, acts], out_rows, n, size,
            tiles + g_tile, 3 * product,
        )
        state = [mixed, back]
        down_grads.append(scatter(*parts))
    mixed_out = lax.psum_scatter(mixed, "tensor", scatter_dimension=0)

    state, up_grads = [], []
    for c in range(chunks):
        grad, *parts = call(
            functools.partial(end_kernel, cfg(c), len(out_rows)), table, offs,
            [full_tokens, back], ups[c], state, [feats], out_rows, n, size,
            tiles + g_tile, 2 * product,
        )
        state = [grad]
        up_grads.append(scatter(*parts))
    grad_tokens = lax.psum_scatter(grad, "tensor", scatter_dimension=0)

    def join(grads):
        return jnp.concatenate([sum(g[1:], g[0]) for g in grads], axis=0)

    return mixed_out, grad_tokens, join(up_grads), join(down_grads)


def solution(mesh):
    in_specs = (
        P(("group", "dp"), "tensor"),
        P(("group", "dp"), "tensor"),
        P("tensor", "dp", None),
        P("tensor", "dp", None),
        P("tensor", None),
        P("tensor", None),
        P("tensor"),
    )
    out_specs = (
        P(("group", "dp"), "tensor"),
        P(("group", "dp"), "tensor"),
        P(("group", "tensor"), "dp", None),
        P(("group", "tensor"), "dp", None),
    )
    return jax.shard_map(
        functools.partial(on_device, mesh.shape["group"], mesh.shape["dp"]),
        mesh=mesh, in_specs=in_specs, out_specs=out_specs, check_vma=False,
    )
```

time: 974 us -> 531 us (0.55)
  matrix products: 411 us -> 0 us
  waiting for transfers between devices: 521 us -> 343 us
  Pallas kernels: 0 us -> 122 us
  starting transfers between devices: 0.32 us -> 22.9 us
  other arithmetic: 0.01 us -> 10.5 us
    dot_general x14 -> x0, matrix products: 411 us -> none  [the longest x1 62.8 us: on_device(): jnp.einsum('tsb,tse->sbe', picked, grad_upper, precision=precise)]
    ppermute x0 -> x32, waiting for transfers between devices: none -> 342 us  [the longest x8 274 us: over_x(): return lax.ppermute(v, 'dp', [(0, 2), (2, 0), (1, 3), (3, 1)])]
    all_gather x4 -> x2, waiting for transfers between devices: 275 us -> 0.02 us  [the longest x1 0.02 us: on_device(): full_cot = lax.all_gather(cotangent, 'tensor')]
    reduce_scatter x4 -> x2, waiting for transfers between devices: 244 us -> 0.01 us  [the longest x1 0.01 us: on_device(): grad_tokens = lax.psum_scatter(grad, 'tensor', scatter_dimension=0)]
    pallas_call x0 -> x6, Pallas kernels: none -> 122 us  [call(): pl.pallas_call(kernel, grid_spec=pltpu.PrefetchScalarGridSpec(num_scalar_...]
    ppermute x0 -> x32, starting transfers between devices: none -> 22.6 us  [the longest x8 11.7 us: over_x(): return lax.ppermute(v, 'dp', [(0, 2), (2, 0), (1, 3), (3, 1)])]
    unnamed x12 -> x52, local copies, waits for them, and re-layouts: 22.1 us -> 4.57 us
  transfers between devices with their start and end apart: 8 -> 36, of which waited for: 6 -> 17; matrix products, arithmetic and copies ran while one was open for 38% -> 4% of each run, Pallas kernels for 0% -> 11%
where the time goes in v1:
time: 531 us; the launch traced here: 530 us
  waiting for transfers between devices  343 us (65%)
  Pallas kernels  122 us (23%)
  starting transfers between devices  22.9 us (4%)
  local copies, waits for them, and re-layouts  16.6 us (3%)
  between operations  14.7 us (3%)
  other arithmetic  10.5 us (2%)
    ppermute x8, waiting for transfers between devices, over_x(): return lax.ppermute(v, 'dp', [(0, 2), (2, 0), (1, 3), (3, 1)])  274 us
    pallas_call x6, Pallas kernels, call(): pl.pallas_call(kernel, grid_spec=pltpu.PrefetchScalarGridSpec(num_scalar_...  122 us
    ppermute x4, waiting for transfers between devices, over_y(): return lax.ppermute(v, 'group', [(0, 1), (1, 0)])  54.6 us
    ppermute x20, waiting for transfers between devices, over_core(): return lax.ppermute(v, 'dp', [(0, 1), (1, 0), (2, 3), (3, 2)])  13.6 us
    ppermute x8, starting transfers between devices, over_x(): return lax.ppermute(v, 'dp', [(0, 2), (2, 0), (1, 3), (3, 1)])  11.7 us
  transfers between devices with their start and end apart: 36, of which 17 were waited for; matrix products, arithmetic and copies ran while one was open for 4% of the time, Pallas kernels for 11%

profile of v1, /device:TPU:0, one launch (start us, length us, event | category | flops | bytes accessed | tf_op | source)
XLA Modules:
  0.0 529.8 jit_solution(5078216711618098329)
XLA Ops:
  8.0 2.9 fusion.1
  12.4 3.0 collective-permute-start.6
  15.7 5.1 fusion
  26.6 15.7 %collective-permute-done.6.refs_2_ = f32[36,32,256]{2,1,0:T(8,128)} collective-permute-done((f32[36,32,256]{2,1,0:T(8,128)S(1)}, f32[36,32,256]{2,1,0:T(8,128)}, u32[]{:S(2)}, u32[]{:S(2)}) %collective-permute-start.6) | collective-permute-done | bytes 1179680 | tf_op jit(solution)/shard_map/ppermute | solution.py:217
  44.4 23.1 %collective-permute-done.1.refs_2_ = f32[36,32,256]{2,1,0:T(8,128)S(1)} collective-permute-done((f32[36,32,256]{2,1,0:T(8,128)S(1)}, f32[36,32,256]{2,1,0:T(8,128)S(1)}, u32[]{:S(2)}, u32[]{:S(2)}) %collective-permute-start.1) | collective-permute-done | bytes 1179680 | tf_op jit(solution)/shard_map/ppermute | solution.py:217
  67.5 25.3 %collective-permute-done.16.refs_2_ = f32[36,32,256]{2,1,0:T(8,128)S(1)} collective-permute-done((f32[36,32,256]{2,1,0:T(8,128)S(1)}, f32[36,32,256]{2,1,0:T(8,128)S(1)}, u32[]{:S(2)}, u32[]{:S(2)}) %collective-permute-start.16) | collective-permute-done | bytes 1179680 | tf_op jit(solution)/shard_map/ppermute | solution.py:217
  92.8 24.6 %collective-permute-done.11.refs_2_ = f32[36,32,256]{2,1,0:T(8,128)} collective-permute-done((f32[36,32,256]{2,1,0:T(8,128)S(1)}, f32[36,32,256]{2,1,0:T(8,128)}, u32[]{:S(2)}, u32[]{:S(2)}) %collective-permute-start.11) | collective-permute-done | bytes 1179680 | tf_op jit(solution)/shard_map/ppermute | solution.py:217
  119.7 26.6 %collective-permute-done.2.refs_3_ = f32[36,32,256]{2,1,0:T(8,128)} collective-permute-done((f32[36,32,256]{2,1,0:T(8,128)S(1)}, f32[36,32,256]{2,1,0:T(8,128)}, u32[]{:S(2)}, u32[]{:S(2)}) %collective-permute-start.2) | collective-permute-done | bytes 1179680 | tf_op jit(solution)/shard_map/ppermute | solution.py:220
  148.7 22.9 %collective-permute-done.17.refs_3_ = f32[36,32,256]{2,1,0:T(8,128)} collective-permute-done((f32[36,32,256]{2,1,0:T(8,128)S(1)}, f32[36,32,256]{2,1,0:T(8,128)}, u32[]{:S(2)}, u32[]{:S(2)}) %collective-permute-start.17) | collective-permute-done | bytes 1179680 | tf_op jit(solution)/shard_map/ppermute | solution.py:220
  176.2 13.8 %shard_map.105.refs_6_ = f32[16,240,256]{2,1,0:T(8,128)} custom-call(s32[3,72]{1,0:T(4,128)} %add_add_fusion.4.table, s32[10]{0:T(128)} %stack.41.offs, f32[4,240,1024]{2,1,0:T(8,128)} %bitcast.13, f32[36,64,256]{2,1,0:T(8,128)} %copy-done.1, f32[36,64,256]{2,1,0:T(8,128)} %copy-done.7, f32[36,32,256]{2,1,0:T(8,128)} %collective-permute-done.6.refs_2_, ...), custom_call_target="tpu_custom_call" | custom-call | flops 3397386240 | bytes 17301504 | tf_op jit(solution)/shard_map/pallas_call | solution.py:174
  190.0 5.1 collective-permute-done.12.refs_3_
  196.1 18.8 %shard_map.106 = (f32[16,240,256]{2,1,0:T(8,128)}, f32[16,240,256]{2,1,0:T(8,128)}) custom-call(s32[3,72]{1,0:T(4,128)} %add_add_fusion.4.table, s32[10]{0:T(128)} %stack.41.offs, f32[4,240,1024]{2,1,0:T(8,128)} %bitcast.14, f32[36,64,256]{2,1,0:T(8,128)} %copy-done, f32[36,64,256]{2,1,0:T(8,128)} %copy-done.8, f32[36,32,256]{2,1,0:T(8,128)} %copy-done.13, ...), custom_call_target="tpu_custom_call" | custom-call | flops 3397386240 | bytes 25165824 | tf_op jit(solution)/shard_map/pallas_call | solution.py:174
  214.9 23.4 %shard_map.107 = (f32[4,240,1024]{2,1,0:T(8,128)}, f32[16,240,256]{2,1,0:T(8,128)}, f32[36,64,256]{2,1,0:T(8,128)}, f32[36,64,256]{2,1,0:T(8,128)}, f32[36,64,256]{2,1,0:T(8,128)}, /*index=5*/f32[36,64,256]{2,1,0:T(8,128)}) custom-call(s32[3,72]{1,0:T(4,128)} %add_add_fusion.4.table, s32[10]{0:T(128)} %stack.41.offs, f32[16,240,256]{2,1,0:T(8,128)} %get-tuple-element.28.act, ...), custom_call_target="tpu_custom_call" | custom-call | flops 10192158720 | bytes 38535168 | tf_op jit(solution)/shard_map/pallas_call | solution.py:174
  239.4 26.5 %shard_map.108 = (f32[4,240,1024]{2,1,0:T(8,128)}, f32[16,240,256]{2,1,0:T(8,128)}, f32[36,64,256]{2,1,0:T(8,128)}, f32[36,64,256]{2,1,0:T(8,128)}, f32[36,64,256]{2,1,0:T(8,128)}, /*index=5*/f32[36,64,256]{2,1,0:T(8,128)}) custom-call(s32[3,72]{1,0:T(4,128)} %add_add_fusion.4.table, s32[10]{0:T(128)} %stack.41.offs, f32[16,240,256]{2,1,0:T(8,128)} %get-tuple-element.28.act, ...), custom_call_target="tpu_custom_call" | custom-call | flops 10192158720 | bytes 46399488 | tf_op jit(solution)/shard_map/pallas_call | solution.py:174
  265.9 19.3 %shard_map.109 = (f32[4,240,1024]{2,1,0:T(8,128)}, f32[36,64,256]{2,1,0:T(8,128)}, f32[36,64,256]{2,1,0:T(8,128)}, f32[36,64,256]{2,1,0:T(8,128)}, f32[36,64,256]{2,1,0:T(8,128)}) custom-call(s32[3,72]{1,0:T(4,128)} %add_add_fusion.4.table, s32[10]{0:T(128)} %stack.41.offs, f32[4,240,1024]{2,1,0:T(8,128)} %bitcast.15, f32[16,240,256]{2,1,0:T(8,128)} %get-tuple-element.33.gh, ...), custom_call_target="tpu_custom_call" | custom-call | flops 6794772480 | bytes 30670848 | tf_op jit(solution)/shard_map/pallas_call | solution.py:174
  285.2 20.5 %shard_map.110 = (f32[4,240,1024]{2,1,0:T(8,128)}, f32[36,64,256]{2,1,0:T(8,128)}, f32[36,64,256]{2,1,0:T(8,128)}, f32[36,64,256]{2,1,0:T(8,128)}, f32[36,64,256]{2,1,0:T(8,128)}) custom-call(s32[3,72]{1,0:T(4,128)} %add_add_fusion.4.table, s32[10]{0:T(128)} %stack.41.offs, f32[4,240,1024]{2,1,0:T(8,128)} %bitcast.16, f32[16,240,256]{2,1,0:T(8,128)} %get-tuple-element.33.gh, ...), custom_call_target="tpu_custom_call" | custom-call | flops 6794772480 | bytes 34603008 | tf_op jit(solution)/shard_map/pallas_call | solution.py:174
  307.8 3.4 collective-permute-done.27
  321.7 3.0 collective-permute-done.24
  328.4 40.2 %collective-permute-done.28 = f32[36,64,256]{2,1,0:T(8,128)S(1)} collective-permute-done((f32[36,64,256]{2,1,0:T(8,128)S(1)}, f32[36,64,256]{2,1,0:T(8,128)S(1)}, u32[]{:S(2)}, u32[]{:S(2)}) %collective-permute-start.28) | collective-permute-done | bytes 2359328 | tf_op jit(solution)/shard_map/ppermute | solution.py:217
  370.7 48.4 %collective-permute-done.31 = f32[36,64,256]{2,1,0:T(8,128)S(1)} collective-permute-done((f32[36,64,256]{2,1,0:T(8,128)S(1)}, f32[36,64,256]{2,1,0:T(8,128)S(1)}, u32[]{:S(2)}, u32[]{:S(2)}) %collective-permute-start.31) | collective-permute-done | bytes 2359328 | tf_op jit(solution)/shard_map/ppermute | solution.py:217
  419.9 2.7 pad_maximum_fusion.1
  422.6 47.1 %collective-permute-done.22 = f32[36,64,256]{2,1,0:T(8,128)S(1)} collective-permute-done((f32[36,64,256]{2,1,0:T(8,128)S(1)}, f32[36,64,256]{2,1,0:T(8,128)S(1)}, u32[]{:S(2)}, u32[]{:S(2)}) %collective-permute-start.22) | collective-permute-done | bytes 2359328 | tf_op jit(solution)/shard_map/ppermute | solution.py:217
  470.5 49.2 %collective-permute-done.25 = f32[36,64,256]{2,1,0:T(8,128)S(1)} collective-permute-done((f32[36,64,256]{2,1,0:T(8,128)S(1)}, f32[36,64,256]{2,1,0:T(8,128)S(1)}, u32[]{:S(2)}, u32[]{:S(2)}) %collective-permute-start.25) | collective-permute-done | bytes 2359328 | tf_op jit(solution)/shard_map/ppermute | solution.py:217
  520.5 2.7 pad_maximum_fusion
  (129 shorter events, 41.8 us)
Async XLA Ops:
  7.2 169.0 %all-gather.5.cloned.1.call-start = ((), (), s32[]{:S(2)}) async-start(), calls=%async_computation.4 | async-start | bytes 4915200 | tf_op jit(solution)/shard_map/all_gather | solution.py:257
  7.9 207.0 %all-gather.7.cloned.1.call-start = ((), (), s32[]{:S(2)}) async-start(), calls=%async_computation.5 | async-start | bytes 4915200 | tf_op jit(solution)/shard_map/all_gather | solution.py:260
  15.5 507.8 %reduce-scatter.5.cloned.1.call-start = ((), (), s32[]{:S(2)}) async-start(), calls=%async_computation.3 | async-start | bytes 4915200 | tf_op jit(solution)/shard_map/reduce_scatter | solution.py:301
  15.6 51.9 %collective-permute-start.1 = (f32[36,32,256]{2,1,0:T(8,128)S(1)}, f32[36,32,256]{2,1,0:T(8,128)S(1)}, u32[]{:S(2)}, u32[]{:S(2)}) collective-permute-start(f32[36,32,256]{2,1,0:T(8,128)S(1)} %constant_dynamic-slice_fusion.3), channel_id=1, source_target_pairs={{0,2},{2,0},{1,3},{3,1},{4,6},{6,4},{5,7},{7,5},{8,10},{10,8},{9,1... | collective-permute-start | bytes 3538952 | tf_op jit(solution)/shard_map/ppermute | solution.py:217
  22.5 70.3 %collective-permute-start.16 = (f32[36,32,256]{2,1,0:T(8,128)S(1)}, f32[36,32,256]{2,1,0:T(8,128)S(1)}, u32[]{:S(2)}, u32[]{:S(2)}) collective-permute-start(f32[36,32,256]{2,1,0:T(8,128)S(1)} %constant_dynamic-slice_fusion), channel_id=1, source_target_pairs={{0,2},{2,0},{1,3},{3,1},{4,6},{6,4},{5,7},{7,5},{8,10},{10,8},{9,1... | collective-permute-start | bytes 3538952 | tf_op jit(solution)/shard_map/ppermute | solution.py:217
  24.6 94.9 %collective-permute-start.5 = (f32[36,64,256]{2,1,0:T(8,128)S(1)}, f32[36,64,256]{2,1,0:T(8,128)S(1)}, u32[]{:S(2)}, u32[]{:S(2)}) collective-permute-start(f32[36,64,256]{2,1,0:T(8,128)S(1)} %copy-done.2), channel_id=1, source_target_pairs={{0,1},{1,0},{2,3},{3,2},{4,5},{5,4},{6,7},{7,6},{8,9},{9,8},{10,11... | collective-permute-start | bytes 7077896 | tf_op jit(solution)/shard_map/ppermute | solution.py:214
  26.0 91.3 %collective-permute-start.11 = (f32[36,32,256]{2,1,0:T(8,128)S(1)}, f32[36,32,256]{2,1,0:T(8,128)}, u32[]{:S(2)}, u32[]{:S(2)}) collective-permute-start(f32[36,32,256]{2,1,0:T(8,128)S(1)} %constant_dynamic-slice_fusion.1), channel_id=1, source_target_pairs={{0,2},{2,0},{1,3},{3,1},{4,6},{6,4},{5,7},{7,5},{8,10},{10,8},{9,1... | collective-permute-start | bytes 3538952 | tf_op jit(solution)/shard_map/ppermute | solution.py:217
  42.3 76.8 %collective-permute-start.7 = (f32[36,32,256]{2,1,0:T(8,128)}, f32[36,32,256]{2,1,0:T(8,128)S(1)}, u32[]{:S(2)}, u32[]{:S(2)}) collective-permute-start(f32[36,32,256]{2,1,0:T(8,128)} %collective-permute-done.6.refs_2_), channel_id=1, source_target_pairs={{0,16},{16,0},{1,17},{17,1},{2,18},{18,2},{3,19},{19,3},{4,20},{20... | collective-permute-start | bytes 3538952 | tf_op jit(solution)/shard_map/ppermute | solution.py:220
  67.5 79.4 %collective-permute-start = (f32[36,64,256]{2,1,0:T(8,128)S(1)}, f32[36,64,256]{2,1,0:T(8,128)S(1)}, u32[]{:S(2)}, u32[]{:S(2)}) collective-permute-start(f32[36,64,256]{2,1,0:T(8,128)S(1)} %get-tuple-element.55.refs_0_), channel_id=1, source_target_pairs={{0,1},{1,0},{2,3},{3,2},{4,5},{5,4},{6,7},{7,6},{8,9},{9,8},{10,11... | collective-permute-start | bytes 7077896 | tf_op jit(solution)/shard_map/ppermute | solution.py:214
  119.1 52.5 %collective-permute-start.17 = (f32[36,32,256]{2,1,0:T(8,128)S(1)}, f32[36,32,256]{2,1,0:T(8,128)}, u32[]{:S(2)}, u32[]{:S(2)}) collective-permute-start(f32[36,32,256]{2,1,0:T(8,128)S(1)} %collective-permute-done.16.refs_2_), channel_id=1, source_target_pairs={{0,16},{16,0},{1,17},{17,1},{2,18},{18,2},{3,19},{19,3},{4,20},{20... | collective-permute-start | bytes 3538952 | tf_op jit(solution)/shard_map/ppermute | solution.py:220
  119.5 52.2 %collective-permute-start.18 = (f32[36,32,256]{2,1,0:T(8,128)S(1)}, f32[36,32,256]{2,1,0:T(8,128)S(1)}, u32[]{:S(2)}, u32[]{:S(2)}) collective-permute-start(f32[36,32,256]{2,1,0:T(8,128)S(1)} %collective-permute-done.16.refs_2_), channel_id=1, source_target_pairs={{0,1},{1,0},{2,3},{3,2},{4,5},{5,4},{6,7},{7,6},{8,9},{9,8},{10,11... | collective-permute-start | bytes 3538952 | tf_op jit(solution)/shard_map/ppermute | solution.py:214
  146.4 68.5 %collective-permute-start.15 = (f32[36,64,256]{2,1,0:T(8,128)}, f32[36,64,256]{2,1,0:T(8,128)}, u32[]{:S(2)}, u32[]{:S(2)}) collective-permute-start(f32[36,64,256]{2,1,0:T(8,128)} %get-tuple-element.52.refs_0_), channel_id=1, source_target_pairs={{0,1},{1,0},{2,3},{3,2},{4,5},{5,4},{6,7},{7,6},{8,9},{9,8},{10,11... | collective-permute-start | bytes 7077896 | tf_op jit(solution)/shard_map/ppermute | solution.py:214
  146.9 48.2 %collective-permute-start.12 = (f32[36,32,256]{2,1,0:T(8,128)}, f32[36,32,256]{2,1,0:T(8,128)S(1)}, u32[]{:S(2)}, u32[]{:S(2)}) collective-permute-start(f32[36,32,256]{2,1,0:T(8,128)} %collective-permute-done.11.refs_2_), channel_id=1, source_target_pairs={{0,16},{16,0},{1,17},{17,1},{2,18},{18,2},{3,19},{19,3},{4,20},{20... | collective-permute-start | bytes 3538952 | tf_op jit(solution)/shard_map/ppermute | solution.py:220
  171.7 66.7 %collective-permute-start.10 = (f32[36,64,256]{2,1,0:T(8,128)}, f32[36,64,256]{2,1,0:T(8,128)}, u32[]{:S(2)}, u32[]{:S(2)}) collective-permute-start(f32[36,64,256]{2,1,0:T(8,128)} %get-tuple-element.53.refs_0_), channel_id=1, source_target_pairs={{0,1},{1,0},{2,3},{3,2},{4,5},{5,4},{6,7},{7,6},{8,9},{9,8},{10,11... | collective-permute-start | bytes 7077896 | tf_op jit(solution)/shard_map/ppermute | solution.py:214
  173.7 41.2 %collective-permute-start.19 = (f32[36,32,256]{2,1,0:T(8,128)}, f32[36,32,256]{2,1,0:T(8,128)}, u32[]{:S(2)}, u32[]{:S(2)}) collective-permute-start(f32[36,32,256]{2,1,0:T(8,128)} %collective-permute-done.17.refs_3_), channel_id=1, source_target_pairs={{0,1},{1,0},{2,3},{3,2},{4,5},{5,4},{6,7},{7,6},{8,9},{9,8},{10,11... | collective-permute-start | bytes 3538952 | tf_op jit(solution)/shard_map/ppermute | solution.py:214
  195.1 43.3 %collective-permute-start.13 = (f32[36,32,256]{2,1,0:T(8,128)}, f32[36,32,256]{2,1,0:T(8,128)S(1)}, u32[]{:S(2)}, u32[]{:S(2)}) collective-permute-start(f32[36,32,256]{2,1,0:T(8,128)} %collective-permute-done.11.refs_2_), channel_id=1, source_target_pairs={{0,1},{1,0},{2,3},{3,2},{4,5},{5,4},{6,7},{7,6},{8,9},{9,8},{10,11... | collective-permute-start | bytes 3538952 | tf_op jit(solution)/shard_map/ppermute | solution.py:214
  195.1 43.3 %collective-permute-start.14 = (f32[36,32,256]{2,1,0:T(8,128)S(1)}, f32[36,32,256]{2,1,0:T(8,128)}, u32[]{:S(2)}, u32[]{:S(2)}) collective-permute-start(f32[36,32,256]{2,1,0:T(8,128)S(1)} %collective-permute-done.12.refs_3_), channel_id=1, source_target_pairs={{0,1},{1,0},{2,3},{3,2},{4,5},{5,4},{6,7},{7,6},{8,9},{9,8},{10,11... | collective-permute-start | bytes 3538952 | tf_op jit(solution)/shard_map/ppermute | solution.py:214
  305.7 217.6 %reduce-scatter.3.cloned.1.call-start = ((), (), s32[]{:S(2)}) async-start(), calls=%async_computation.2 | async-start | bytes 4915200 | tf_op jit(solution)/shard_map/reduce_scatter | solution.py:290
  314.5 54.1 %collective-permute-start.28 = (f32[36,64,256]{2,1,0:T(8,128)S(1)}, f32[36,64,256]{2,1,0:T(8,128)S(1)}, u32[]{:S(2)}, u32[]{:S(2)}) collective-permute-start(f32[36,64,256]{2,1,0:T(8,128)S(1)} %add.92), channel_id=1, source_target_pairs={{0,2},{2,0},{1,3},{3,1},{4,6},{6,4},{5,7},{7,5},{8,10},{10,8},{9,1... | collective-permute-start | bytes 7077896 | tf_op jit(solution)/shard_map/ppermute | solution.py:217
  317.9 101.3 %collective-permute-start.31 = (f32[36,64,256]{2,1,0:T(8,128)S(1)}, f32[36,64,256]{2,1,0:T(8,128)S(1)}, u32[]{:S(2)}, u32[]{:S(2)}) collective-permute-start(f32[36,64,256]{2,1,0:T(8,128)S(1)} %add.95), channel_id=1, source_target_pairs={{0,2},{2,0},{1,3},{3,1},{4,6},{6,4},{5,7},{7,5},{8,10},{10,8},{9,1... | collective-permute-start | bytes 7077896 | tf_op jit(solution)/shard_map/ppermute | solution.py:217
  321.3 101.3 %collective-permute-start.20 = (f32[36,64,256]{2,1,0:T(8,128)}, f32[36,64,256]{2,1,0:T(8,128)S(1)}, u32[]{:S(2)}, u32[]{:S(2)}) collective-permute-start(f32[36,64,256]{2,1,0:T(8,128)} %get-tuple-element.37), channel_id=1, source_target_pairs={{0,1},{1,0},{2,3},{3,2},{4,5},{5,4},{6,7},{7,6},{8,9},{9,8},{10,11... | collective-permute-start | bytes 7077896 | tf_op jit(solution)/shard_map/ppermute | solution.py:214
  324.7 145.1 %collective-permute-start.22 = (f32[36,64,256]{2,1,0:T(8,128)S(1)}, f32[36,64,256]{2,1,0:T(8,128)S(1)}, u32[]{:S(2)}, u32[]{:S(2)}) collective-permute-start(f32[36,64,256]{2,1,0:T(8,128)S(1)} %add.86), channel_id=1, source_target_pairs={{0,2},{2,0},{1,3},{3,1},{4,6},{6,4},{5,7},{7,5},{8,10},{10,8},{9,1... | collective-permute-start | bytes 7077896 | tf_op jit(solution)/shard_map/ppermute | solution.py:217
  328.0 142.5 %collective-permute-start.23 = (f32[36,64,256]{2,1,0:T(8,128)S(1)}, f32[36,64,256]{2,1,0:T(8,128)S(1)}, u32[]{:S(2)}, u32[]{:S(2)}) collective-permute-start(f32[36,64,256]{2,1,0:T(8,128)S(1)} %copy-done.21), channel_id=1, source_target_pairs={{0,1},{1,0},{2,3},{3,2},{4,5},{5,4},{6,7},{7,6},{8,9},{9,8},{10,11... | collective-permute-start | bytes 7077896 | tf_op jit(solution)/shard_map/ppermute | solution.py:214
  368.6 151.1 %collective-permute-start.25 = (f32[36,64,256]{2,1,0:T(8,128)S(1)}, f32[36,64,256]{2,1,0:T(8,128)S(1)}, u32[]{:S(2)}, u32[]{:S(2)}) collective-permute-start(f32[36,64,256]{2,1,0:T(8,128)S(1)} %add.89), channel_id=1, source_target_pairs={{0,2},{2,0},{1,3},{3,1},{4,6},{6,4},{5,7},{7,5},{8,10},{10,8},{9,1... | collective-permute-start | bytes 7077896 | tf_op jit(solution)/shard_map/ppermute | solution.py:217
  (38 other events, 1192.7 us)
Sparse Core Ops, SparseCore 0:
  9.6 79.1 all-gather.4
  90.3 74.9 all-gather.6
  305.8 73.9 reduce-scatter.4
  382.5 72.9 reduce-scatter.2

commit v2 on v1

--- a/solution.py
+++ b/solution.py
@@ -158,17 +158,18 @@
         place[...] += live * mm(b, tile, 1, 1)
 
 
-def call(kernel, table, offs, whole_in, pieces, inits, whole_out, out_rows, n, size, scratch, flops):
-    slots = pieces[0].shape[0]
+def call(kernel, table, offs, whole_in, pieces, inits, whole_out, out_rows, n, size, scratch, flops,
+         lo, slots):
+    skip = lo // n
 
     def whole(shape):
         return pl.BlockSpec(shape, lambda i, *_: (0,) * len(shape), pipeline_mode=pl.Buffered(1))
 
-    def part(rows):
-        return pl.BlockSpec((n, rows, size), lambda i, *_: (i, 0, 0))
+    def part(rows, ahead=0):
+        return pl.BlockSpec((n, rows, size), lambda i, *_: (i + ahead, 0, 0))
 
     args = list(whole_in) + list(pieces) + list(inits)
-    moved = sum(a.size for a in args) * 4 + 4 * sum(
+    moved = sum(a.size for a in list(whole_in) + list(inits)) * 4 + 4 * slots * size * size + 4 * sum(
         slots * rows * size for rows in out_rows
     ) + 4 * sum(functools.reduce(lambda x, y: x * y, s) for s in whole_out)
     return pl.pallas_call(
@@ -177,7 +178,7 @@
             num_scalar_prefetch=2,
             grid=(slots // n,),
             in_specs=[whole(a.shape) for a in whole_in]
-            + [part(p.shape[1]) for p in pieces]
+            + [part(p.shape[1], skip) for p in pieces]
             + [whole(a.shape) for a in inits],
             out_specs=[whole(s) for s in whole_out] + [part(rows) for rows in out_rows],
             scratch_shapes=scratch,
@@ -197,10 +198,13 @@
     tensor = lax.axis_size("tensor")
     per = width // size
     hidden = FF // (size * tensor)
-    paired = groups == 2 and dps == 4 and slots % 8 == 0
+    paired = groups == 2 and dps == 4 and slots % 24 == 0
     chunks = 2 if paired else 1
     count = slots // chunks
-    n = max(k for k in (1, 2, 3, 4) if count % k == 0)
+    n = max(k for k in (1, 2, 3, 4) if (count // 3 if paired else count) % k == 0)
+
+    def after(value, *others):
+        return lax.optimization_barrier((value, *others))[0]
 
     table = jnp.stack([block_col[0], block_row[0], jnp.broadcast_to(block_count, (slots,))])
     d = lax.axis_index("dp")
@@ -219,11 +223,13 @@
         def over_y(v):
             return lax.ppermute(v, "group", [(0, 1), (1, 0)])
 
-        def gather(w):
+        def gather(w, *ahead):
             near = lax.dynamic_slice_in_dim(w, y * half, half, axis=1)
-            by_x = over_x(near)
+            return (w, over_core(w), over_x(after(near, *ahead)))
+
+        def spread(w, by_core, by_x):
             by_y = over_y(by_x)
-            return (w, over_core(w), by_x, by_y, over_core(by_x), over_core(by_y))
+            return (w, by_core, by_x, by_y, over_core(by_x), by_y)
 
         offs = jnp.stack(
             [
@@ -236,74 +242,97 @@
                 d * rows_w,
                 other_x * rows_w,
                 other_core * rows_w,
-                other_both * rows_w,
             ]
+            + [other_both * rows_w + k * (rows_w // 4) for k in range(4)]
         ).astype(jnp.int32)
-        out_rows = (rows_w,) * 4
-
-        def scatter(mine, to_x, to_core, to_both):
-            far = over_x(to_x + over_core(to_both))
-            return mine + over_core(to_core), far
+        out_rows = (rows_w,) * 3 + (rows_w // 4,) * 4
+
+        def scatter(mine, to_x, to_core, *to_both):
+            summed = to_x + jnp.concatenate([over_core(v) for v in to_both], axis=1)
+            return summed, (over_x(summed), mine, over_core(to_core))
     else:
         offs = jnp.zeros((2,), jnp.int32)
         out_rows = (size,)
 
-        def gather(w):
+        def gather(w, *ahead):
             return (lax.all_gather(w, "dp", axis=1, tiled=True),)
 
+        def spread(whole):
+            return (whole,)
+
         def scatter(whole):
-            return (lax.psum_scatter(whole, "dp", scatter_dimension=1, tiled=True),)
+            return whole, (lax.psum_scatter(whole, "dp", scatter_dimension=1, tiled=True),)
 
     full_tokens = lax.all_gather(tokens, "tensor")
     ups = [gather(w_up[c * count:(c + 1) * count]) for c in range(chunks)]
-    downs = [gather(w_down[c * count:(c + 1) * count]) for c in range(chunks)]
+    downs = [gather(w_down[c * count:(c + 1) * count], ups[c][-1]) for c in range(chunks)]
     full_cot = lax.all_gather(cotangent, "tensor")
 
     acts = (hidden, rows, size)
     feats = (tensor, rows, width)
     tiles = [pltpu.VMEM((n, size, size), BF16), pltpu.VMEM((n, size, size), BF16)]
     g_tile = [pltpu.VMEM((n, size, size), F32)]
-    product = 6 * count * rows * size * size
-
-    def cfg(c):
-        return (c * count, n, per, size, len(ups[c]), c == 0, c == chunks - 1)
-
+    product = 6 * rows * size * size
+
+    def cfg(c, lo, first, last):
+        return (c * count + lo, n, per, size, len(ups[0]), first, last)
+
+    ups, downs = [spread(*u) for u in ups], [spread(*u) for u in downs]
+    if paired:
+        ups = [(*u[:-1], over_core(u[-1])) for u in ups]
     state = []
     for c in range(chunks):
         last = c == chunks - 1
         state = call(
-            functools.partial(up_kernel, cfg(c)), table, offs, [full_tokens], ups[c], state,
-            [acts, acts] if last else [acts], (), n, size,
-            tiles + ([pltpu.VMEM(acts, F32)] if last else []), product,
+            functools.partial(up_kernel, cfg(c, 0, c == 0, last)),
+            after(table, downs[c][2]) if paired else table, offs, [full_tokens],
+            ups[c], state, [acts, acts] if last else [acts], (), n, size,
+            tiles + ([pltpu.VMEM(acts, F32)] if last else []), count * product, 0, count,
         )
     act, slope = state
-
-    state, down_grads = [], []
-    for c in range(chunks):
+    if paired:
+        downs = [(*u[:-1], over_core(after(u[-1], act))) for u in downs]
+
+    sums, sent = [], []
+
+    def gate():
+        waits = sums[-1:] + [g[0] for g in sent[-2:-1]]
+        return after(table, *(waits or downs[-1][1:])) if paired else table
+
+    third = count // 3
+    whole = [(c, 0, count) for c in range(chunks)]
+    cuts = [(0, 0, third), (0, third, count - third)] + whole[1:] if paired else whole
+    state = []
+    for c, lo, num in cuts:
+        last = c == chunks - 1
         mixed, back, *parts = call(
-            functools.partial(down_kernel, cfg(c), len(out_rows)), table, offs,
-            [act, slope, full_cot], downs[c], state, [feats, acts], out_rows, n, size,
-            tiles + g_tile, 3 * product,
+            functools.partial(down_kernel, cfg(c, lo, not state, last), len(out_rows)),
+            gate(), offs, [act, slope, full_cot], downs[c], state, [feats, acts], out_rows, n, size,
+            tiles + g_tile, 3 * num * product, lo, num,
         )
         state = [mixed, back]
-        down_grads.append(scatter(*parts))
+        summed, grads = scatter(*parts)
+        sums.append(summed)
+        sent.append(grads)
     mixed_out = lax.psum_scatter(mixed, "tensor", scatter_dimension=0)
 
-    state, up_grads = [], []
-    for c in range(chunks):
+    state = []
+    for c, lo, num in cuts:
         grad, *parts = call(
-            functools.partial(end_kernel, cfg(c), len(out_rows)), table, offs,
-            [full_tokens, back], ups[c], state, [feats], out_rows, n, size,
-            tiles + g_tile, 2 * product,
+            functools.partial(end_kernel, cfg(c, lo, not state, False), len(out_rows)),
+            gate(), offs, [full_tokens, back], ups[c], state, [feats], out_rows, n, size,
+            tiles + g_tile, 2 * num * product, lo, num,
         )
         state = [grad]
-        up_grads.append(scatter(*parts))
+        summed, grads = scatter(*parts)
+        sums.append(summed)
+        sent.append(grads)
     grad_tokens = lax.psum_scatter(grad, "tensor", scatter_dimension=0)
 
     def join(grads):
         return jnp.concatenate([sum(g[1:], g[0]) for g in grads], axis=0)
 
-    return mixed_out, grad_tokens, join(up_grads), join(down_grads)
+    return mixed_out, grad_tokens, join(sent[len(cuts):]), join(sent[:len(cuts)])
 
 
 def solution(mesh):

time: 531 us -> 516 us (0.972)
  waiting for transfers between devices: 343 us -> 292 us
  Pallas kernels: 122 us -> 142 us
  other arithmetic: 10.5 us -> 19.2 us
  starting transfers between devices: 22.9 us -> 28.4 us
    ppermute x4, waiting for transfers between devices: 54.6 us -> 16.5 us  [over_y(): return lax.ppermute(v, 'group', [(0, 1), (1, 0)])]
    ppermute x8 -> x10, waiting for transfers between devices: 274 us -> 251 us  [over_x(): return lax.ppermute(v, 'dp', [(0, 2), (2, 0), (1, 3), (3, 1)])]
    pallas_call x6 -> x8, Pallas kernels: 122 us -> 142 us  [call(): pl.pallas_call(kernel, grid_spec=pltpu.PrefetchScalarGridSpec(num_scalar_...]
    ppermute x20 -> x42, waiting for transfers between devices: 13.6 us -> 23.6 us  [over_core(): return lax.ppermute(v, 'dp', [(0, 1), (1, 0), (2, 3), (3, 2)])]
    add x4 -> x6, other arithmetic: 1.47 us -> 8.75 us  [scatter(): summed = to_x + jnp.concatenate([over_core(v) for v in to_both], axis=1)]
    ppermute x8 -> x10, starting transfers between devices: 11.7 us -> 13.5 us  [over_x(): return lax.ppermute(v, 'dp', [(0, 2), (2, 0), (1, 3), (3, 1)])]
  transfers between devices with their start and end apart: 36 -> 60, of which waited for: 17 -> 36; matrix products, arithmetic and copies ran while one was open for 4% -> 5% of each run, Pallas kernels for 11% -> 20%
where the time goes in v2:
time: 516 us; the launch traced here: 514 us
  waiting for transfers between devices  292 us (57%)
  Pallas kernels  142 us (28%)
  starting transfers between devices  28.4 us (6%)
  other arithmetic  19.2 us (4%)
  local copies, waits for them, and re-layouts  18.5 us (4%)
  between operations  14.9 us (3%)
    ppermute x10, waiting for transfers between devices, over_x(): return lax.ppermute(v, 'dp', [(0, 2), (2, 0), (1, 3), (3, 1)])  251 us
    pallas_call x8, Pallas kernels, call(): pl.pallas_call(kernel, grid_spec=pltpu.PrefetchScalarGridSpec(num_scalar_...  142 us
    ppermute x42, waiting for transfers between devices, over_core(): return lax.ppermute(v, 'dp', [(0, 1), (1, 0), (2, 3), (3, 2)])  23.6 us
    ppermute x4, waiting for transfers between devices, over_y(): return lax.ppermute(v, 'group', [(0, 1), (1, 0)])  16.5 us
    ppermute x10, starting transfers between devices, over_x(): return lax.ppermute(v, 'dp', [(0, 2), (2, 0), (1, 3), (3, 1)])  13.5 us
  transfers between devices with their start and end apart: 60, of which 36 were waited for; matrix products, arithmetic and copies ran while one was open for 5% of the time, Pallas kernels for 20%

profile of v2, /device:TPU:0, one launch (start us, length us, event | category | flops | bytes accessed | tf_op | source)
XLA Modules:
  0.0 514.5 jit_solution(16695485720840140690)
XLA Ops:
  8.0 2.8 fusion
  10.9 3.0 collective-permute-start.9
  15.5 2.9 fusion.1
  21.3 19.4 %collective-permute-done.9.refs_2_ = f32[36,32,256]{2,1,0:T(8,128)S(1)} collective-permute-done((f32[36,32,256]{2,1,0:T(8,128)S(1)}, f32[36,32,256]{2,1,0:T(8,128)S(1)}, u32[]{:S(2)}, u32[]{:S(2)}) %collective-permute-start.9) | collective-permute-done | bytes 1179680 | tf_op jit(solution)/shard_map/ppermute | solution.py:221
  44.7 21.4 %collective-permute-done.1.refs_2_ = f32[36,32,256]{2,1,0:T(8,128)} collective-permute-done((f32[36,32,256]{2,1,0:T(8,128)}, f32[36,32,256]{2,1,0:T(8,128)}, u32[]{:S(2)}, u32[]{:S(2)}) %collective-permute-start.1) | collective-permute-done | bytes 1179680 | tf_op jit(solution)/shard_map/ppermute | solution.py:221
  66.1 24.4 %collective-permute-done.10.refs_2_ = f32[36,32,256]{2,1,0:T(8,128)} collective-permute-done((f32[36,32,256]{2,1,0:T(8,128)}, f32[36,32,256]{2,1,0:T(8,128)}, u32[]{:S(2)}, u32[]{:S(2)}) %collective-permute-start.10) | collective-permute-done | bytes 1179680 | tf_op jit(solution)/shard_map/ppermute | solution.py:221
  94.3 23.7 %collective-permute-done.2.refs_2_ = f32[36,32,256]{2,1,0:T(8,128)} collective-permute-done((f32[36,32,256]{2,1,0:T(8,128)}, f32[36,32,256]{2,1,0:T(8,128)}, u32[]{:S(2)}, u32[]{:S(2)}) %collective-permute-start.2) | collective-permute-done | bytes 1179680 | tf_op jit(solution)/shard_map/ppermute | solution.py:221
  124.4 13.9 %shard_map.105.refs_6_ = f32[16,240,256]{2,1,0:T(8,128)} custom-call(s32[3,72]{1,0:T(4,128)} %add_add_fusion.6.table, s32[13]{0:T(128)} %stack.53.offs, f32[4,240,1024]{2,1,0:T(8,128)} %bitcast.16, f32[36,64,256]{2,1,0:T(8,128)} %copy-done, f32[36,64,256]{2,1,0:T(8,128)} %collective-permute-done.11.refs_1_, f32[36,32,256]{2,1,0:T(8,128)} %copy-done.3, ...), custom_call_target="tpu_custom_call" | custom-call | flops 3397386240 | bytes 17301504 | tf_op jit(solution)/shard_map/pallas_call | solution.py:175
  138.6 18.8 %shard_map.106 = (f32[16,240,256]{2,1,0:T(8,128)}, f32[16,240,256]{2,1,0:T(8,128)}) custom-call(s32[3,72]{1,0:T(4,128)} %add_add_fusion.6.table, s32[13]{0:T(128)} %stack.53.offs, f32[4,240,1024]{2,1,0:T(8,128)} %bitcast.17, f32[36,64,256]{2,1,0:T(8,128)} %copy-done.2, f32[36,64,256]{2,1,0:T(8,128)} %copy-done.13, ...), custom_call_target="tpu_custom_call" | custom-call | flops 3397386240 | bytes 25165824 | tf_op jit(solution)/shard_map/pallas_call | solution.py:175
  157.7 15.4 %collective-permute-done.17.refs_3_ = f32[36,32,256]{2,1,0:T(8,128)S(1)} collective-permute-done((f32[36,32,256]{2,1,0:T(8,128)}, f32[36,32,256]{2,1,0:T(8,128)S(1)}, u32[]{:S(2)}, u32[]{:S(2)}) %collective-permute-start.17) | collective-permute-done | bytes 1179680 | tf_op jit(solution)/shard_map/ppermute | solution.py:224
  178.6 14.2 %shard_map.107 = (f32[4,240,1024]{2,1,0:T(8,128)}, f32[16,240,256]{2,1,0:T(8,128)}, f32[12,64,256]{2,1,0:T(8,128)}, f32[12,64,256]{2,1,0:T(8,128)}, f32[12,64,25...) custom-call(s32[3,72]{1,0:T(4,128)} %add_add_fusion.6.table, ...), custom_call_target="tpu_custom_call" | custom-call | flops 3397386240 | bytes 25952256 | tf_op jit(solution)/shard_map/pallas_call | solution.py:175
  197.3 21.1 %shard_map.108 = (f32[4,240,1024]{2,1,0:T(8,128)}, f32[16,240,256]{2,1,0:T(8,128)}, f32[24,64,256]{2,1,0:T(8,128)}, f32[24,64,256]{2,1,0:T(8,128)}, f32[24,64,25...) custom-call(s32[3,72]{1,0:T(4,128)} %add_add_fusion.6.table, ...), custom_call_target="tpu_custom_call" | custom-call | flops 6794772480 | bytes 40108032 | tf_op jit(solution)/shard_map/pallas_call | solution.py:175
  222.1 2.8 maximum_add_fusion.2
  224.9 26.5 %shard_map.109 = (f32[4,240,1024]{2,1,0:T(8,128)}, f32[16,240,256]{2,1,0:T(8,128)}, f32[36,64,256]{2,1,0:T(8,128)}, f32[36,64,256]{2,1,0:T(8,128)}, f32[36,64,25...) custom-call(s32[3,72]{1,0:T(4,128)} %add_add_fusion.6.table, ...), custom_call_target="tpu_custom_call" | custom-call | flops 10192158720 | bytes 46399488 | tf_op jit(solution)/shard_map/pallas_call | solution.py:175
  259.3 84.7 %collective-permute-done.33 = f32[24,64,256]{2,1,0:T(8,128)} collective-permute-done((f32[24,64,256]{2,1,0:T(8,128)S(1)}, f32[24,64,256]{2,1,0:T(8,128)}, u32[]{:S(2)}, u32[]{:S(2)}) %collective-permute-start.33) | collective-permute-done | bytes 1572896 | tf_op jit(solution)/shard_map/ppermute | solution.py:221
  343.9 10.9 %shard_map.110 = (f32[4,240,1024]{2,1,0:T(8,128)}, f32[12,64,256]{2,1,0:T(8,128)}, f32[12,64,256]{2,1,0:T(8,128)}, f32[12,64,256]{2,1,0:T(8,128)}, f32[12,16,256...) custom-call(s32[3,72]{1,0:T(4,128)} %add_add_fusion.6.table, ...), custom_call_target="tpu_custom_call" | custom-call | flops 2264924160 | bytes 18087936 | tf_op jit(solution)/shard_map/pallas_call | solution.py:175
  360.2 16.2 %shard_map.111 = (f32[4,240,1024]{2,1,0:T(8,128)}, f32[24,64,256]{2,1,0:T(8,128)}, f32[24,64,256]{2,1,0:T(8,128)}, f32[24,64,256]{2,1,0:T(8,128)}, f32[24,16,256...) custom-call(s32[3,72]{1,0:T(4,128)} %add_add_fusion.6.table, ...), custom_call_target="tpu_custom_call" | custom-call | flops 4529848320 | bytes 28311552 | tf_op jit(solution)/shard_map/pallas_call | solution.py:175
  380.1 2.8 maximum_add_fusion.3
  383.9 20.4 %shard_map.112 = (f32[4,240,1024]{2,1,0:T(8,128)}, f32[36,64,256]{2,1,0:T(8,128)}, f32[36,64,256]{2,1,0:T(8,128)}, f32[36,64,256]{2,1,0:T(8,128)}, f32[36,16,256...) custom-call(s32[3,72]{1,0:T(4,128)} %add_add_fusion.6.table, ...), custom_call_target="tpu_custom_call" | custom-call | flops 6794772480 | bytes 34603008 | tf_op jit(solution)/shard_map/pallas_call | solution.py:175
  407.6 3.0 collective-permute-done.49
  410.7 4.1 collective-permute-done.50
  422.9 2.8 pad_maximum_fusion.1
  425.7 77.2 %collective-permute-done.45 = f32[24,64,256]{2,1,0:T(8,128)S(1)} collective-permute-done((f32[24,64,256]{2,1,0:T(8,128)S(1)}, f32[24,64,256]{2,1,0:T(8,128)S(1)}, u32[]{:S(2)}, u32[]{:S(2)}) %collective-permute-start.45) | collective-permute-done | bytes 1572896 | tf_op jit(solution)/shard_map/ppermute | solution.py:221
  505.2 2.8 pad_maximum_fusion
  (194 shorter events, 64.6 us)
Async XLA Ops:
  7.2 117.2 %all-gather.5.cloned.1.call-start = ((), (), s32[]{:S(2)}) async-start(), calls=%async_computation.4 | async-start | bytes 4915200 | tf_op jit(solution)/shard_map/all_gather | solution.py:266
  7.9 169.1 %all-gather.7.cloned.1.call-start = ((), (), s32[]{:S(2)}) async-start(), calls=%async_computation.5 | async-start | bytes 4915200 | tf_op jit(solution)/shard_map/all_gather | solution.py:269
  10.9 29.8 %collective-permute-start.9 = (f32[36,32,256]{2,1,0:T(8,128)S(1)}, f32[36,32,256]{2,1,0:T(8,128)S(1)}, u32[]{:S(2)}, u32[]{:S(2)}) collective-permute-start(f32[36,32,256]{2,1,0:T(8,128)S(1)} %constant_dynamic-slice_fusion), channel_id=1, source_target_pairs={{0,2},{2,0},{1,3},{3,1},{4,6},{6,4},{5,7},{7,5},{8,10},{10,8},{9,1... | collective-permute-start | bytes 3538952 | tf_op jit(solution)/shard_map/ppermute | solution.py:221
  15.0 51.0 %collective-permute-start.1 = (f32[36,32,256]{2,1,0:T(8,128)}, f32[36,32,256]{2,1,0:T(8,128)}, u32[]{:S(2)}, u32[]{:S(2)}) collective-permute-start(f32[36,32,256]{2,1,0:T(8,128)} %constant_dynamic-slice_fusion.2), channel_id=1, source_target_pairs={{0,2},{2,0},{1,3},{3,1},{4,6},{6,4},{5,7},{7,5},{8,10},{10,8},{9,1... | collective-permute-start | bytes 3538952 | tf_op jit(solution)/shard_map/ppermute | solution.py:221
  40.7 49.8 %collective-permute-start.10 = (f32[36,32,256]{2,1,0:T(8,128)}, f32[36,32,256]{2,1,0:T(8,128)}, u32[]{:S(2)}, u32[]{:S(2)}) collective-permute-start(f32[36,32,256]{2,1,0:T(8,128)} %get-tuple-element.71), channel_id=1, source_target_pairs={{0,2},{2,0},{1,3},{3,1},{4,6},{6,4},{5,7},{7,5},{8,10},{10,8},{9,1... | collective-permute-start | bytes 3538952 | tf_op jit(solution)/shard_map/ppermute | solution.py:221
  42.8 51.1 %collective-permute-start.11 = (f32[36,64,256]{2,1,0:T(8,128)S(1)}, f32[36,64,256]{2,1,0:T(8,128)}, u32[]{:S(2)}, u32[]{:S(2)}) collective-permute-start(f32[36,64,256]{2,1,0:T(8,128)S(1)} %get-tuple-element.134.refs_0_), channel_id=1, source_target_pairs={{0,1},{1,0},{2,3},{3,2},{4,5},{5,4},{6,7},{7,6},{8,9},{9,8},{10,11... | collective-permute-start | bytes 7077896 | tf_op jit(solution)/shard_map/ppermute | solution.py:218
  42.8 465.1 %reduce-scatter.3.cloned.1.call-start = ((), (), s32[]{:S(2)}) async-start(), calls=%async_computation.2 | async-start | bytes 4915200 | tf_op jit(solution)/shard_map/reduce_scatter | solution.py:317
  42.8 49.4 %collective-permute-start.12 = (f32[36,32,256]{2,1,0:T(8,128)S(1)}, f32[36,32,256]{2,1,0:T(8,128)S(1)}, u32[]{:S(2)}, u32[]{:S(2)}) collective-permute-start(f32[36,32,256]{2,1,0:T(8,128)S(1)} %collective-permute-done.9.refs_2_), channel_id=1, source_target_pairs={{0,16},{16,0},{1,17},{17,1},{2,18},{18,2},{3,19},{19,3},{4,20},{20... | collective-permute-start | bytes 3538952 | tf_op jit(solution)/shard_map/ppermute | solution.py:224
  44.4 49.4 %collective-permute-start.13 = (f32[36,32,256]{2,1,0:T(8,128)S(1)}, f32[36,32,256]{2,1,0:T(8,128)S(1)}, u32[]{:S(2)}, u32[]{:S(2)}) collective-permute-start(f32[36,32,256]{2,1,0:T(8,128)S(1)} %collective-permute-done.9.refs_2_), channel_id=1, source_target_pairs={{0,1},{1,0},{2,3},{3,2},{4,5},{5,4},{6,7},{7,6},{8,9},{9,8},{10,11... | collective-permute-start | bytes 3538952 | tf_op jit(solution)/shard_map/ppermute | solution.py:218
  66.1 54.7 %collective-permute-start.5 = (f32[36,64,256]{2,1,0:T(8,128)}, f32[36,64,256]{2,1,0:T(8,128)S(1)}, u32[]{:S(2)}, u32[]{:S(2)}) collective-permute-start(f32[36,64,256]{2,1,0:T(8,128)} %copy-done.2), channel_id=1, source_target_pairs={{0,1},{1,0},{2,3},{3,2},{4,5},{5,4},{6,7},{7,6},{8,9},{9,8},{10,11... | collective-permute-start | bytes 7077896 | tf_op jit(solution)/shard_map/ppermute | solution.py:218
  90.5 27.5 %collective-permute-start.2 = (f32[36,32,256]{2,1,0:T(8,128)}, f32[36,32,256]{2,1,0:T(8,128)}, u32[]{:S(2)}, u32[]{:S(2)}) collective-permute-start(f32[36,32,256]{2,1,0:T(8,128)} %get-tuple-element.69), channel_id=1, source_target_pairs={{0,2},{2,0},{1,3},{3,1},{4,6},{6,4},{5,7},{7,5},{8,10},{10,8},{9,1... | collective-permute-start | bytes 3538952 | tf_op jit(solution)/shard_map/ppermute | solution.py:221
  93.8 27.4 %collective-permute-start.14 = (f32[36,32,256]{2,1,0:T(8,128)S(1)}, f32[36,32,256]{2,1,0:T(8,128)S(1)}, u32[]{:S(2)}, u32[]{:S(2)}) collective-permute-start(f32[36,32,256]{2,1,0:T(8,128)S(1)} %collective-permute-done.12.refs_3_), channel_id=1, source_target_pairs={{0,1},{1,0},{2,3},{3,2},{4,5},{5,4},{6,7},{7,6},{8,9},{9,8},{10,11... | collective-permute-start | bytes 3538952 | tf_op jit(solution)/shard_map/ppermute | solution.py:218
  118.0 55.0 %collective-permute-start = (f32[36,64,256]{2,1,0:T(8,128)}, f32[36,64,256]{2,1,0:T(8,128)}, u32[]{:S(2)}, u32[]{:S(2)}) collective-permute-start(f32[36,64,256]{2,1,0:T(8,128)} %copy-done.7), channel_id=1, source_target_pairs={{0,1},{1,0},{2,3},{3,2},{4,5},{5,4},{6,7},{7,6},{8,9},{9,8},{10,11... | collective-permute-start | bytes 7077896 | tf_op jit(solution)/shard_map/ppermute | solution.py:218
  119.2 38.3 %collective-permute-start.3 = (f32[36,32,256]{2,1,0:T(8,128)}, f32[36,32,256]{2,1,0:T(8,128)}, u32[]{:S(2)}, u32[]{:S(2)}) collective-permute-start(f32[36,32,256]{2,1,0:T(8,128)} %collective-permute-done.2.refs_2_), channel_id=1, source_target_pairs={{0,16},{16,0},{1,17},{17,1},{2,18},{18,2},{3,19},{19,3},{4,20},{20... | collective-permute-start | bytes 3538952 | tf_op jit(solution)/shard_map/ppermute | solution.py:224
  120.8 52.3 %collective-permute-start.17 = (f32[36,32,256]{2,1,0:T(8,128)}, f32[36,32,256]{2,1,0:T(8,128)S(1)}, u32[]{:S(2)}, u32[]{:S(2)}) collective-permute-start(f32[36,32,256]{2,1,0:T(8,128)} %collective-permute-done.10.refs_2_), channel_id=1, source_target_pairs={{0,16},{16,0},{1,17},{17,1},{2,18},{18,2},{3,19},{19,3},{4,20},{20... | collective-permute-start | bytes 3538952 | tf_op jit(solution)/shard_map/ppermute | solution.py:224
  122.2 52.4 %collective-permute-start.16 = (f32[36,64,256]{2,1,0:T(8,128)}, f32[36,64,256]{2,1,0:T(8,128)}, u32[]{:S(2)}, u32[]{:S(2)}) collective-permute-start(f32[36,64,256]{2,1,0:T(8,128)} %copy-done.1), channel_id=1, source_target_pairs={{0,1},{1,0},{2,3},{3,2},{4,5},{5,4},{6,7},{7,6},{8,9},{9,8},{10,11... | collective-permute-start | bytes 7077896 | tf_op jit(solution)/shard_map/ppermute | solution.py:218
  138.2 35.3 %collective-permute-start.4 = (f32[36,32,256]{2,1,0:T(8,128)}, f32[36,32,256]{2,1,0:T(8,128)S(1)}, u32[]{:S(2)}, u32[]{:S(2)}) collective-permute-start(f32[36,32,256]{2,1,0:T(8,128)} %collective-permute-done.2.refs_2_), channel_id=1, source_target_pairs={{0,1},{1,0},{2,3},{3,2},{4,5},{5,4},{6,7},{7,6},{8,9},{9,8},{10,11... | collective-permute-start | bytes 3538952 | tf_op jit(solution)/shard_map/ppermute | solution.py:218
  196.6 28.3 %collective-permute-start.28 = (f32[12,64,256]{2,1,0:T(8,128)S(1)}, f32[12,64,256]{2,1,0:T(8,128)S(1)}, u32[]{:S(2)}, u32[]{:S(2)}) collective-permute-start(f32[12,64,256]{2,1,0:T(8,128)S(1)} %maximum_add_fusion.4), channel_id=1, source_target_pairs={{0,2},{2,0},{1,3},{3,1},{4,6},{6,4},{5,7},{7,5},{8,10},{10,8},{9,1... | collective-permute-start | bytes 2359304 | tf_op jit(solution)/shard_map/ppermute | solution.py:221
  251.4 256.5 %reduce-scatter.5.cloned.1.call-start = ((), (), s32[]{:S(2)}) async-start(), calls=%async_computation.3 | async-start | bytes 4915200 | tf_op jit(solution)/shard_map/reduce_scatter | solution.py:330
  256.8 103.4 %collective-permute-start.38 = (f32[36,64,256]{2,1,0:T(8,128)S(1)}, f32[36,64,256]{2,1,0:T(8,128)S(1)}, u32[]{:S(2)}, u32[]{:S(2)}) collective-permute-start(f32[36,64,256]{2,1,0:T(8,128)S(1)} %maximum_add_fusion), channel_id=1, source_target_pairs={{0,2},{2,0},{1,3},{3,1},{4,6},{6,4},{5,7},{7,5},{8,10},{10,8},{9,1... | collective-permute-start | bytes 7077896 | tf_op jit(solution)/shard_map/ppermute | solution.py:221
  258.3 85.7 %collective-permute-start.33 = (f32[24,64,256]{2,1,0:T(8,128)S(1)}, f32[24,64,256]{2,1,0:T(8,128)}, u32[]{:S(2)}, u32[]{:S(2)}) collective-permute-start(f32[24,64,256]{2,1,0:T(8,128)S(1)} %copy-done.21), channel_id=1, source_target_pairs={{0,2},{2,0},{1,3},{3,1},{4,6},{6,4},{5,7},{7,5},{8,10},{10,8},{9,1... | collective-permute-start | bytes 4718600 | tf_op jit(solution)/shard_map/ppermute | solution.py:221
  414.7 88.5 %collective-permute-start.52 = (f32[36,64,256]{2,1,0:T(8,128)}, f32[36,64,256]{2,1,0:T(8,128)S(1)}, u32[]{:S(2)}, u32[]{:S(2)}) collective-permute-start(f32[36,64,256]{2,1,0:T(8,128)} %get-tuple-element.127), channel_id=1, source_target_pairs={{0,1},{1,0},{2,3},{3,2},{4,5},{5,4},{6,7},{7,6},{8,9},{9,8},{10,11... | collective-permute-start | bytes 7077896 | tf_op jit(solution)/shard_map/ppermute | solution.py:218
  415.9 87.4 %collective-permute-start.51 = (f32[36,64,256]{2,1,0:T(8,128)S(1)}, f32[36,64,256]{2,1,0:T(8,128)S(1)}, u32[]{:S(2)}, u32[]{:S(2)}) collective-permute-start(f32[36,64,256]{2,1,0:T(8,128)S(1)} %maximum_add_fusion.1), channel_id=1, source_target_pairs={{0,2},{2,0},{1,3},{3,1},{4,6},{6,4},{5,7},{7,5},{8,10},{10,8},{9,1... | collective-permute-start | bytes 7077896 | tf_op jit(solution)/shard_map/ppermute | solution.py:221
  417.0 85.9 %collective-permute-start.45 = (f32[24,64,256]{2,1,0:T(8,128)S(1)}, f32[24,64,256]{2,1,0:T(8,128)S(1)}, u32[]{:S(2)}, u32[]{:S(2)}) collective-permute-start(f32[24,64,256]{2,1,0:T(8,128)S(1)} %copy-done.20), channel_id=1, source_target_pairs={{0,2},{2,0},{1,3},{3,1},{4,6},{6,4},{5,7},{7,5},{8,10},{10,8},{9,1... | collective-permute-start | bytes 4718600 | tf_op jit(solution)/shard_map/ppermute | solution.py:221
  (68 other events, 750.9 us)
Sparse Core Ops, SparseCore 0:
  9.6 79.1 all-gather.4
  90.3 75.0 all-gather.6
  251.5 73.8 reduce-scatter.2
  404.4 72.9 reduce-scatter.4

commit v3 on v2

--- a/solution.py
+++ b/solution.py
@@ -200,6 +200,7 @@
     hidden = FF // (size * tensor)
     paired = groups == 2 and dps == 4 and slots % 24 == 0
     chunks = 2 if paired else 1
+    sums, sent = [], []
     count = slots // chunks
     n = max(k for k in (1, 2, 3, 4) if (count // 3 if paired else count) % k == 0)
 
@@ -249,7 +250,8 @@
 
         def scatter(mine, to_x, to_core, *to_both):
             summed = to_x + jnp.concatenate([over_core(v) for v in to_both], axis=1)
-            return summed, (over_x(summed), mine, over_core(to_core))
+            ahead = [g[0] for g in sent[-1:]]
+            return summed, (over_x(after(summed, *ahead)), mine, over_core(to_core))
     else:
         offs = jnp.zeros((2,), jnp.int32)
         out_rows = (size,)
@@ -292,8 +294,6 @@
     act, slope = state
     if paired:
         downs = [(*u[:-1], over_core(after(u[-1], act))) for u in downs]
-
-    sums, sent = [], []
 
     def gate():
         waits = sums[-1:] + [g[0] for g in sent[-2:-1]]
@@ -317,7 +317,7 @@
     mixed_out = lax.psum_scatter(mixed, "tensor", scatter_dimension=0)
 
     state = []
-    for c, lo, num in cuts:
+    for c, lo, num in whole:
         grad, *parts = call(
             functools.partial(end_kernel, cfg(c, lo, not state, False), len(out_rows)),
             gate(), offs, [full_tokens, back], ups[c], state, [feats], out_rows, n, size,

time: 516 us -> 481 us (0.932)
  waiting for transfers between devices: 292 us -> 265 us
  Pallas kernels: 142 us -> 134 us
    ppermute x10 -> x9, waiting for transfers between devices: 251 us -> 228 us  [over_x(): return lax.ppermute(v, 'dp', [(0, 2), (2, 0), (1, 3), (3, 1)])]
    pallas_call x8 -> x7, Pallas kernels: 142 us -> 134 us  [call(): pl.pallas_call(kernel, grid_spec=pltpu.PrefetchScalarGridSpec(num_scalar_...]
    ppermute x42 -> x37, waiting for transfers between devices: 23.6 us -> 21.1 us  [over_core(): return lax.ppermute(v, 'dp', [(0, 1), (1, 0), (2, 3), (3, 2)])]
    ppermute x10 -> x9, starting transfers between devices: 13.5 us -> 13.4 us  [over_x(): return lax.ppermute(v, 'dp', [(0, 2), (2, 0), (1, 3), (3, 1)])]
  transfers between devices with their start and end apart: 60 -> 54, of which waited for: 36 -> 32; matrix products, arithmetic and copies ran while one was open for 5% -> 7% of each run, Pallas kernels for 20% -> 19%
where the time goes in v3:
time: 481 us; the launch traced here: 479 us
  waiting for transfers between devices  265 us (55%)
  Pallas kernels  134 us (28%)
  starting transfers between devices  26.8 us (6%)
  local copies, waits for them, and re-layouts  19.3 us (4%)
  other arithmetic  19 us (4%)
  between operations  14.7 us (3%)
    ppermute x9, waiting for transfers between devices, over_x(): return lax.ppermute(v, 'dp', [(0, 2), (2, 0), (1, 3), (3, 1)])  228 us
    pallas_call x7, Pallas kernels, call(): pl.pallas_call(kernel, grid_spec=pltpu.PrefetchScalarGridSpec(num_scalar_...  134 us
    ppermute x37, waiting for transfers between devices, over_core(): return lax.ppermute(v, 'dp', [(0, 1), (1, 0), (2, 3), (3, 2)])  21.1 us
    ppermute x4, waiting for transfers between devices, over_y(): return lax.ppermute(v, 'group', [(0, 1), (1, 0)])  15.5 us
    ppermute x9, starting transfers between devices, over_x(): return lax.ppermute(v, 'dp', [(0, 2), (2, 0), (1, 3), (3, 1)])  13.4 us
  transfers between devices with their start and end apart: 54, of which 32 were waited for; matrix products, arithmetic and copies ran while one was open for 7% of the time, Pallas kernels for 19%

profile of v3, /device:TPU:0, one launch (start us, length us, event | category | flops | bytes accessed | tf_op | source)
XLA Modules:
  0.0 479.3 jit_solution(14886626148007393382)
XLA Ops:
  8.0 4.4 fusion
  12.3 2.2 constant_dynamic-slice_fusion
  14.6 3.0 collective-permute-start.9
  18.7 3.3 fusion.1
  24.3 20.1 %collective-permute-done.9.refs_2_ = f32[36,32,256]{2,1,0:T(8,128)S(1)} collective-permute-done((f32[36,32,256]{2,1,0:T(8,128)S(1)}, f32[36,32,256]{2,1,0:T(8,128)S(1)}, u32[]{:S(2)}, u32[]{:S(2)}) %collective-permute-start.9) | collective-permute-done | bytes 1179680 | tf_op jit(solution)/shard_map/ppermute | solution.py:222
  49.3 20.4 %collective-permute-done.1.refs_2_ = f32[36,32,256]{2,1,0:T(8,128)} collective-permute-done((f32[36,32,256]{2,1,0:T(8,128)}, f32[36,32,256]{2,1,0:T(8,128)}, u32[]{:S(2)}, u32[]{:S(2)}) %collective-permute-start.1) | collective-permute-done | bytes 1179680 | tf_op jit(solution)/shard_map/ppermute | solution.py:222
  69.8 24.3 %collective-permute-done.10.refs_2_ = f32[36,32,256]{2,1,0:T(8,128)S(1)} collective-permute-done((f32[36,32,256]{2,1,0:T(8,128)}, f32[36,32,256]{2,1,0:T(8,128)S(1)}, u32[]{:S(2)}, u32[]{:S(2)}) %collective-permute-start.10) | collective-permute-done | bytes 1179680 | tf_op jit(solution)/shard_map/ppermute | solution.py:222
  97.9 23.7 %collective-permute-done.2.refs_2_ = f32[36,32,256]{2,1,0:T(8,128)} collective-permute-done((f32[36,32,256]{2,1,0:T(8,128)}, f32[36,32,256]{2,1,0:T(8,128)}, u32[]{:S(2)}, u32[]{:S(2)}) %collective-permute-start.2) | collective-permute-done | bytes 1179680 | tf_op jit(solution)/shard_map/ppermute | solution.py:222
  129.1 13.9 %shard_map.105.refs_6_ = f32[16,240,256]{2,1,0:T(8,128)} custom-call(s32[3,72]{1,0:T(4,128)} %add_add_fusion.5.table, s32[13]{0:T(128)} %stack.53.offs, f32[4,240,1024]{2,1,0:T(8,128)} %bitcast.19, f32[36,64,256]{2,1,0:T(8,128)} %get-tuple-element.124.refs_0_, f32[36,64,256]{2,1,0:T(8,128)} %collective-permute-done.11.refs_1_, f32[36,32,256]{2,1,0:T(8,128)} %copy-done.12, ...), custom_call_target="tpu_custom_call" | custom-call | flops 3397386240 | bytes 17301504 | tf_op jit(solution)/shard_map/pallas_call | solution.py:175
  143.4 18.8 %shard_map.106 = (f32[16,240,256]{2,1,0:T(8,128)}, f32[16,240,256]{2,1,0:T(8,128)}) custom-call(s32[3,72]{1,0:T(4,128)} %add_add_fusion.5.table, s32[13]{0:T(128)} %stack.53.offs, f32[4,240,1024]{2,1,0:T(8,128)} %bitcast.20, f32[36,64,256]{2,1,0:T(8,128)} %copy-done.1, f32[36,64,256]{2,1,0:T(8,128)} %copy-done.5, ...), custom_call_target="tpu_custom_call" | custom-call | flops 3397386240 | bytes 25165824 | tf_op jit(solution)/shard_map/pallas_call | solution.py:175
  162.4 14.3 %collective-permute-done.17.refs_3_ = f32[36,32,256]{2,1,0:T(8,128)} collective-permute-done((f32[36,32,256]{2,1,0:T(8,128)S(1)}, f32[36,32,256]{2,1,0:T(8,128)}, u32[]{:S(2)}, u32[]{:S(2)}) %collective-permute-start.17) | collective-permute-done | bytes 1179680 | tf_op jit(solution)/shard_map/ppermute | solution.py:225
  181.6 14.2 %shard_map.107 = (f32[4,240,1024]{2,1,0:T(8,128)}, f32[16,240,256]{2,1,0:T(8,128)}, f32[12,64,256]{2,1,0:T(8,128)}, f32[12,64,256]{2,1,0:T(8,128)}, f32[12,64,25...) custom-call(s32[3,72]{1,0:T(4,128)} %add_add_fusion.5.table, ...), custom_call_target="tpu_custom_call" | custom-call | flops 3397386240 | bytes 25952256 | tf_op jit(solution)/shard_map/pallas_call | solution.py:175
  200.2 21.1 %shard_map.108 = (f32[4,240,1024]{2,1,0:T(8,128)}, f32[16,240,256]{2,1,0:T(8,128)}, f32[24,64,256]{2,1,0:T(8,128)}, f32[24,64,256]{2,1,0:T(8,128)}, f32[24,64,25...) custom-call(s32[3,72]{1,0:T(4,128)} %add_add_fusion.5.table, ...), custom_call_target="tpu_custom_call" | custom-call | flops 6794772480 | bytes 40108032 | tf_op jit(solution)/shard_map/pallas_call | solution.py:175
  225.0 2.8 maximum_add_fusion.3
  227.8 26.4 %shard_map.109 = (f32[4,240,1024]{2,1,0:T(8,128)}, f32[16,240,256]{2,1,0:T(8,128)}, f32[36,64,256]{2,1,0:T(8,128)}, f32[36,64,256]{2,1,0:T(8,128)}, f32[36,64,25...) custom-call(s32[3,72]{1,0:T(4,128)} %add_add_fusion.5.table, ...), custom_call_target="tpu_custom_call" | custom-call | flops 10192158720 | bytes 46399488 | tf_op jit(solution)/shard_map/pallas_call | solution.py:175
  261.1 30.3 %collective-permute-done.33 = f32[24,64,256]{2,1,0:T(8,128)} collective-permute-done((f32[24,64,256]{2,1,0:T(8,128)}, f32[24,64,256]{2,1,0:T(8,128)}, u32[]{:S(2)}, u32[]{:S(2)}) %collective-permute-start.33) | collective-permute-done | bytes 1572896 | tf_op jit(solution)/shard_map/ppermute | solution.py:222
  292.7 19.3 %shard_map.110 = (f32[4,240,1024]{2,1,0:T(8,128)}, f32[36,64,256]{2,1,0:T(8,128)}, f32[36,64,256]{2,1,0:T(8,128)}, f32[36,64,256]{2,1,0:T(8,128)}, f32[36,16,256...) custom-call(s32[3,72]{1,0:T(4,128)} %add_add_fusion.5.table, ...), custom_call_target="tpu_custom_call" | custom-call | flops 6794772480 | bytes 30670848 | tf_op jit(solution)/shard_map/pallas_call | solution.py:175
  318.9 24.8 %collective-permute-done.38 = f32[36,64,256]{2,1,0:T(8,128)S(1)} collective-permute-done((f32[36,64,256]{2,1,0:T(8,128)S(1)}, f32[36,64,256]{2,1,0:T(8,128)S(1)}, u32[]{:S(2)}, u32[]{:S(2)}) %collective-permute-start.38) | collective-permute-done | bytes 2359328 | tf_op jit(solution)/shard_map/ppermute | solution.py:222
  343.8 20.4 %shard_map.111 = (f32[4,240,1024]{2,1,0:T(8,128)}, f32[36,64,256]{2,1,0:T(8,128)}, f32[36,64,256]{2,1,0:T(8,128)}, f32[36,64,256]{2,1,0:T(8,128)}, f32[36,16,256...) custom-call(s32[3,72]{1,0:T(4,128)} %add_add_fusion.5.table, ...), custom_call_target="tpu_custom_call" | custom-call | flops 6794772480 | bytes 34603008 | tf_op jit(solution)/shard_map/pallas_call | solution.py:175
  369.7 4.1 collective-permute-done.44
  376.1 39.7 %collective-permute-done.39 = f32[36,64,256]{2,1,0:T(8,128)S(1)} collective-permute-done((f32[36,64,256]{2,1,0:T(8,128)S(1)}, f32[36,64,256]{2,1,0:T(8,128)S(1)}, u32[]{:S(2)}, u32[]{:S(2)}) %collective-permute-start.39) | collective-permute-done | bytes 2359328 | tf_op jit(solution)/shard_map/ppermute | solution.py:222
  421.2 2.8 pad_maximum_fusion.1
  424.6 44.8 %collective-permute-done.45 = f32[36,64,256]{2,1,0:T(8,128)S(1)} collective-permute-done((f32[36,64,256]{2,1,0:T(8,128)S(1)}, f32[36,64,256]{2,1,0:T(8,128)S(1)}, u32[]{:S(2)}, u32[]{:S(2)}) %collective-permute-start.45) | collective-permute-done | bytes 2359328 | tf_op jit(solution)/shard_map/ppermute | solution.py:222
  470.1 2.7 pad_maximum_fusion
  (159 shorter events, 62.9 us)
Async XLA Ops:
  7.2 121.9 %all-gather.5.cloned.1.call-start = ((), (), s32[]{:S(2)}) async-start(), calls=%async_computation.4 | async-start | bytes 4915200 | tf_op jit(solution)/shard_map/all_gather | solution.py:268
  7.9 172.7 %all-gather.7.cloned.1.call-start = ((), (), s32[]{:S(2)}) async-start(), calls=%async_computation.5 | async-start | bytes 4915200 | tf_op jit(solution)/shard_map/all_gather | solution.py:271
  14.6 29.8 %collective-permute-start.9 = (f32[36,32,256]{2,1,0:T(8,128)S(1)}, f32[36,32,256]{2,1,0:T(8,128)S(1)}, u32[]{:S(2)}, u32[]{:S(2)}) collective-permute-start(f32[36,32,256]{2,1,0:T(8,128)S(1)} %constant_dynamic-slice_fusion), channel_id=1, source_target_pairs={{0,2},{2,0},{1,3},{3,1},{4,6},{6,4},{5,7},{7,5},{8,10},{10,8},{9,1... | collective-permute-start | bytes 3538952 | tf_op jit(solution)/shard_map/ppermute | solution.py:222
  18.7 51.0 %collective-permute-start.1 = (f32[36,32,256]{2,1,0:T(8,128)}, f32[36,32,256]{2,1,0:T(8,128)}, u32[]{:S(2)}, u32[]{:S(2)}) collective-permute-start(f32[36,32,256]{2,1,0:T(8,128)} %constant_dynamic-slice_fusion.2), channel_id=1, source_target_pairs={{0,2},{2,0},{1,3},{3,1},{4,6},{6,4},{5,7},{7,5},{8,10},{10,8},{9,1... | collective-permute-start | bytes 3538952 | tf_op jit(solution)/shard_map/ppermute | solution.py:222
  45.4 48.7 %collective-permute-start.10 = (f32[36,32,256]{2,1,0:T(8,128)}, f32[36,32,256]{2,1,0:T(8,128)S(1)}, u32[]{:S(2)}, u32[]{:S(2)}) collective-permute-start(f32[36,32,256]{2,1,0:T(8,128)} %get-tuple-element.66), channel_id=1, source_target_pairs={{0,2},{2,0},{1,3},{3,1},{4,6},{6,4},{5,7},{7,5},{8,10},{10,8},{9,1... | collective-permute-start | bytes 3538952 | tf_op jit(solution)/shard_map/ppermute | solution.py:222
  47.5 49.9 %collective-permute-start.11 = (f32[36,64,256]{2,1,0:T(8,128)}, f32[36,64,256]{2,1,0:T(8,128)}, u32[]{:S(2)}, u32[]{:S(2)}) collective-permute-start(f32[36,64,256]{2,1,0:T(8,128)} %get-tuple-element.124.refs_0_), channel_id=1, source_target_pairs={{0,1},{1,0},{2,3},{3,2},{4,5},{5,4},{6,7},{7,6},{8,9},{9,8},{10,11... | collective-permute-start | bytes 7077896 | tf_op jit(solution)/shard_map/ppermute | solution.py:219
  47.5 425.3 %reduce-scatter.3.cloned.1.call-start = ((), (), s32[]{:S(2)}) async-start(), calls=%async_computation.2 | async-start | bytes 4915200 | tf_op jit(solution)/shard_map/reduce_scatter | solution.py:317
  47.5 48.3 %collective-permute-start.12 = (f32[36,32,256]{2,1,0:T(8,128)}, f32[36,32,256]{2,1,0:T(8,128)S(1)}, u32[]{:S(2)}, u32[]{:S(2)}) collective-permute-start(f32[36,32,256]{2,1,0:T(8,128)} %copy-done.12), channel_id=1, source_target_pairs={{0,16},{16,0},{1,17},{17,1},{2,18},{18,2},{3,19},{19,3},{4,20},{20... | collective-permute-start | bytes 3538952 | tf_op jit(solution)/shard_map/ppermute | solution.py:225
  49.1 48.3 %collective-permute-start.13 = (f32[36,32,256]{2,1,0:T(8,128)}, f32[36,32,256]{2,1,0:T(8,128)}, u32[]{:S(2)}, u32[]{:S(2)}) collective-permute-start(f32[36,32,256]{2,1,0:T(8,128)} %copy-done.12), channel_id=1, source_target_pairs={{0,1},{1,0},{2,3},{3,2},{4,5},{5,4},{6,7},{7,6},{8,9},{9,8},{10,11... | collective-permute-start | bytes 3538952 | tf_op jit(solution)/shard_map/ppermute | solution.py:219
  69.7 54.6 %collective-permute-start.5 = (f32[36,64,256]{2,1,0:T(8,128)}, f32[36,64,256]{2,1,0:T(8,128)S(1)}, u32[]{:S(2)}, u32[]{:S(2)}) collective-permute-start(f32[36,64,256]{2,1,0:T(8,128)} %copy-done.1), channel_id=1, source_target_pairs={{0,1},{1,0},{2,3},{3,2},{4,5},{5,4},{6,7},{7,6},{8,9},{9,8},{10,11... | collective-permute-start | bytes 7077896 | tf_op jit(solution)/shard_map/ppermute | solution.py:219
  121.6 55.1 %collective-permute-start = (f32[36,64,256]{2,1,0:T(8,128)}, f32[36,64,256]{2,1,0:T(8,128)}, u32[]{:S(2)}, u32[]{:S(2)}) collective-permute-start(f32[36,64,256]{2,1,0:T(8,128)} %copy-done.2), channel_id=1, source_target_pairs={{0,1},{1,0},{2,3},{3,2},{4,5},{5,4},{6,7},{7,6},{8,9},{9,8},{10,11... | collective-permute-start | bytes 7077896 | tf_op jit(solution)/shard_map/ppermute | solution.py:219
  122.7 39.4 %collective-permute-start.3 = (f32[36,32,256]{2,1,0:T(8,128)}, f32[36,32,256]{2,1,0:T(8,128)}, u32[]{:S(2)}, u32[]{:S(2)}) collective-permute-start(f32[36,32,256]{2,1,0:T(8,128)} %collective-permute-done.2.refs_2_), channel_id=1, source_target_pairs={{0,16},{16,0},{1,17},{17,1},{2,18},{18,2},{3,19},{19,3},{4,20},{20... | collective-permute-start | bytes 3538952 | tf_op jit(solution)/shard_map/ppermute | solution.py:225
  124.3 52.4 %collective-permute-start.17 = (f32[36,32,256]{2,1,0:T(8,128)S(1)}, f32[36,32,256]{2,1,0:T(8,128)}, u32[]{:S(2)}, u32[]{:S(2)}) collective-permute-start(f32[36,32,256]{2,1,0:T(8,128)S(1)} %collective-permute-done.10.refs_2_), channel_id=1, source_target_pairs={{0,16},{16,0},{1,17},{17,1},{2,18},{18,2},{3,19},{19,3},{4,20},{20... | collective-permute-start | bytes 3538952 | tf_op jit(solution)/shard_map/ppermute | solution.py:225
  126.9 50.3 %collective-permute-start.16 = (f32[36,64,256]{2,1,0:T(8,128)S(1)}, f32[36,64,256]{2,1,0:T(8,128)}, u32[]{:S(2)}, u32[]{:S(2)}) collective-permute-start(f32[36,64,256]{2,1,0:T(8,128)S(1)} %get-tuple-element.126.refs_0_), channel_id=1, source_target_pairs={{0,1},{1,0},{2,3},{3,2},{4,5},{5,4},{6,7},{7,6},{8,9},{9,8},{10,11... | collective-permute-start | bytes 7077896 | tf_op jit(solution)/shard_map/ppermute | solution.py:219
  143.0 34.2 %collective-permute-start.4 = (f32[36,32,256]{2,1,0:T(8,128)}, f32[36,32,256]{2,1,0:T(8,128)S(1)}, u32[]{:S(2)}, u32[]{:S(2)}) collective-permute-start(f32[36,32,256]{2,1,0:T(8,128)} %collective-permute-done.2.refs_2_), channel_id=1, source_target_pairs={{0,1},{1,0},{2,3},{3,2},{4,5},{5,4},{6,7},{7,6},{8,9},{9,8},{10,11... | collective-permute-start | bytes 3538952 | tf_op jit(solution)/shard_map/ppermute | solution.py:219
  254.3 218.5 %reduce-scatter.5.cloned.1.call-start = ((), (), s32[]{:S(2)}) async-start(), calls=%async_computation.3 | async-start | bytes 4915200 | tf_op jit(solution)/shard_map/reduce_scatter | solution.py:330
  254.5 36.8 %collective-permute-start.33 = (f32[24,64,256]{2,1,0:T(8,128)}, f32[24,64,256]{2,1,0:T(8,128)}, u32[]{:S(2)}, u32[]{:S(2)}) collective-permute-start(f32[24,64,256]{2,1,0:T(8,128)} %maximum_add_fusion.3), channel_id=1, source_target_pairs={{0,2},{2,0},{1,3},{3,1},{4,6},{6,4},{5,7},{7,5},{8,10},{10,8},{9,1... | collective-permute-start | bytes 4718600 | tf_op jit(solution)/shard_map/ppermute | solution.py:222
  291.3 52.5 %collective-permute-start.38 = (f32[36,64,256]{2,1,0:T(8,128)S(1)}, f32[36,64,256]{2,1,0:T(8,128)S(1)}, u32[]{:S(2)}, u32[]{:S(2)}) collective-permute-start(f32[36,64,256]{2,1,0:T(8,128)S(1)} %maximum_add_fusion), channel_id=1, source_target_pairs={{0,2},{2,0},{1,3},{3,1},{4,6},{6,4},{5,7},{7,5},{8,10},{10,8},{9,1... | collective-permute-start | bytes 7077896 | tf_op jit(solution)/shard_map/ppermute | solution.py:222
  364.2 51.6 %collective-permute-start.39 = (f32[36,64,256]{2,1,0:T(8,128)S(1)}, f32[36,64,256]{2,1,0:T(8,128)S(1)}, u32[]{:S(2)}, u32[]{:S(2)}) collective-permute-start(f32[36,64,256]{2,1,0:T(8,128)S(1)} %maximum_add_fusion.1), channel_id=1, source_target_pairs={{0,2},{2,0},{1,3},{3,1},{4,6},{6,4},{5,7},{7,5},{8,10},{10,8},{9,1... | collective-permute-start | bytes 7077896 | tf_op jit(solution)/shard_map/ppermute | solution.py:222
  366.2 53.4 %collective-permute-start.49 = (f32[36,64,256]{2,1,0:T(8,128)}, f32[36,64,256]{2,1,0:T(8,128)S(1)}, u32[]{:S(2)}, u32[]{:S(2)}) collective-permute-start(f32[36,64,256]{2,1,0:T(8,128)} %get-tuple-element.123), channel_id=1, source_target_pairs={{0,1},{1,0},{2,3},{3,2},{4,5},{5,4},{6,7},{7,6},{8,9},{9,8},{10,11... | collective-permute-start | bytes 7077896 | tf_op jit(solution)/shard_map/ppermute | solution.py:219
  368.8 47.0 %collective-permute-start.47 = (f32[12,64,256]{2,1,0:T(8,128)}, f32[12,64,256]{2,1,0:T(8,128)S(1)}, u32[]{:S(2)}, u32[]{:S(2)}) collective-permute-start(f32[12,64,256]{2,1,0:T(8,128)} %get-tuple-element.119), channel_id=1, source_target_pairs={{0,1},{1,0},{2,3},{3,2},{4,5},{5,4},{6,7},{7,6},{8,9},{9,8},{10,11... | collective-permute-start | bytes 2359304 | tf_op jit(solution)/shard_map/ppermute | solution.py:219
  369.6 47.9 %collective-permute-start.48 = (f32[24,64,256]{2,1,0:T(8,128)}, f32[24,64,256]{2,1,0:T(8,128)S(1)}, u32[]{:S(2)}, u32[]{:S(2)}) collective-permute-start(f32[24,64,256]{2,1,0:T(8,128)} %get-tuple-element.121), channel_id=1, source_target_pairs={{0,1},{1,0},{2,3},{3,2},{4,5},{5,4},{6,7},{7,6},{8,9},{9,8},{10,11... | collective-permute-start | bytes 4718600 | tf_op jit(solution)/shard_map/ppermute | solution.py:219
  373.8 50.2 %collective-permute-start.40 = (f32[36,64,256]{2,1,0:T(8,128)}, f32[36,64,256]{2,1,0:T(8,128)S(1)}, u32[]{:S(2)}, u32[]{:S(2)}) collective-permute-start(f32[36,64,256]{2,1,0:T(8,128)} %get-tuple-element.109), channel_id=1, source_target_pairs={{0,1},{1,0},{2,3},{3,2},{4,5},{5,4},{6,7},{7,6},{8,9},{9,8},{10,11... | collective-permute-start | bytes 7077896 | tf_op jit(solution)/shard_map/ppermute | solution.py:219
  415.8 53.7 %collective-permute-start.45 = (f32[36,64,256]{2,1,0:T(8,128)S(1)}, f32[36,64,256]{2,1,0:T(8,128)S(1)}, u32[]{:S(2)}, u32[]{:S(2)}) collective-permute-start(f32[36,64,256]{2,1,0:T(8,128)S(1)} %maximum_add_fusion.2), channel_id=1, source_target_pairs={{0,2},{2,0},{1,3},{3,1},{4,6},{6,4},{5,7},{7,5},{8,10},{10,8},{9,1... | collective-permute-start | bytes 7077896 | tf_op jit(solution)/shard_map/ppermute | solution.py:222
  (52 other events, 900.3 us)
Sparse Core Ops, SparseCore 0:
  9.6 79.1 all-gather.4
  90.3 74.9 all-gather.6
  254.4 73.8 reduce-scatter.2
  364.3 73.9 reduce-scatter.4
